TPU v7x, 32 devices: a whole 2x2x4 slice. The times are simulated.
32 devices in a mesh: groups: 2 (over y), dp: 2 (over core), mp: 8 (over z, x).
Axes of the slice: x: 2, y: 2, z: 4, core: 2. Of those that a mesh axis runs over, the one named last changes fastest.
Arguments:
- tokens: bfloat16 [768, 6144], P(('groups', 'dp'), 'mp'), parts along dimension 0, may hold values from -6 to 6
- row_image: int32 [768], P(('groups', 'dp')), parts along dimension 0, may hold values from 0 to 10, as said below
- norm_gain: bfloat16 [6144], P('mp'), may hold values from 0.099609375 to 1.8984375
- inner_weight: bfloat16 [6144, 24576], P(('dp', 'mp')), may hold values from -0.078125 to 0.078125
- inner_bias: bfloat16 [24576], P(('dp', 'mp')), may hold values from -3 to 3
- outer_weight: bfloat16 [24576, 6144], P(('dp', 'mp')), may hold values from -0.0546875 to 0.0546875
- outer_bias: bfloat16 [6144], P('mp'), may hold values from -3 to 3
Outputs:
- mixed_rows: bfloat16 [768, 6144], P(('groups', 'dp'), 'mp'), parts along dimension 0
- pooled: float32 [20, 6144], P('groups', 'mp'), parts along dimension 0
There are 2 independent parts, one for each index of `groups`. A program takes and returns all parts, laid end to end along the dimension named above; an argument that names none is the same for every part. Nothing has to cross between parts.
Inputs may be any that keep to these rules, and one draw needn't show every extreme that they name: `row_image`: each data shard's 192 rows hold its images one after another from row 0, image k of a shard starting at row k * 32; an image's rows are consecutive and carry its number, all other rows carry 10. Images are numbered upward through shard 0 and then shard 1, every image has 25 to 32 rows, and the last image of each shard has exactly 32. One shard (the loaded one) holds 6 images, with image rows up to row 191; the other holds 4 images, up to row 127. The loaded shard hands its first 32 rows to the other.
All inputs are finite; a program needn't handle non-finite values.
Results may differ from a plain program's by a relative error of at most 0.0043.
Values may be sent and summed in bfloat16 or wider, within the bound.
No kernel may reach another device: no remote copies, remote signals or barrier semaphores. Data moves between devices by JAX's collectives and lax.ppermute only.
A program may use at most 256 MiB of HBM per device.

v0:
```python
import jax
import jax.numpy as jnp
from jax import lax
from jax.sharding import PartitionSpec as P

D = 6144
SEND = 32
KEEP = 160
IMAGES = 10


epsilon = 1e-06


def partner(array, axis, stride):
    return lax.ppermute(array, axis, [(i, i ^ 1 << stride) for i in range(lax.axis_size(axis))])


def body(tokens, row_image, norm_gain, inner_weight, inner_bias, outer_weight, outer_bias):
    model_parts = lax.axis_size("mp")
    data_parts = lax.axis_size("dp")
    local_cols = tokens.shape[1]
    offset = jnp.where(row_image[KEEP] < IMAGES, SEND, 0).astype(jnp.int32)
    incoming = partner(tokens[:SEND], "dp", 0)
    own_rows = lax.dynamic_slice_in_dim(tokens, offset, KEEP - SEND, 0)
    tail_rows = jnp.where(offset > 0, tokens[KEEP:], incoming)
    work_rows = jnp.concatenate([own_rows, tail_rows], axis=0)
    work_values = work_rows.astype(jnp.float32)
    moments = lax.psum(
        (jnp.sum(work_values, axis=1), jnp.sum(work_values * work_values, axis=1)), "mp"
    )
    row_mean = (moments[0] / D)[:, None]
    row_var = (moments[1] / D)[:, None] - row_mean * row_mean
    own_normed = (
        (work_values - row_mean) * lax.rsqrt(row_var + epsilon) * norm_gain.astype(jnp.float32)
    ).astype(jnp.bfloat16)
    normed = lax.all_gather(own_normed, "mp", axis=1, tiled=True)
    local_weight_rows = inner_weight.shape[0]
    unit_count = inner_weight.shape[1]
    weight_blocks = inner_weight.reshape(
        local_weight_rows, data_parts, model_parts, unit_count // (data_parts * model_parts)
    )
    relaid_rows = lax.all_to_all(weight_blocks, "mp", split_axis=2, concat_axis=0, tiled=True)
    relaid_rows = relaid_rows.reshape(local_weight_rows * model_parts, unit_count // model_parts)
    pre_act = jnp.dot(
        normed,
        lax.all_gather(relaid_rows, "dp", axis=0, tiled=True),
        preferred_element_type=jnp.float32,
    )
    down_rows, bias_units = (
        lax.all_gather(outer_weight, "dp", axis=0, tiled=True),
        lax.all_gather(inner_bias, "dp", axis=0, tiled=True),
    )
    hidden = jax.nn.gelu(pre_act + bias_units.astype(jnp.float32), approximate=False).astype(
        jnp.bfloat16
    )
    partial_out = jnp.dot(hidden, down_rows, preferred_element_type=jnp.float32)
    summed = lax.psum(partial_out, "mp")
    branch_out = lax.dynamic_slice_in_dim(summed, lax.axis_index("mp") * local_cols, local_cols, 1)
    result_rows = (work_values + branch_out + outer_bias.astype(jnp.float32)).astype(jnp.bfloat16)
    returned = partner(result_rows[KEEP - SEND :], "dp", 0)
    row_ids = jnp.arange(tokens.shape[0], dtype=jnp.int32)[:, None]
    placed = lax.dynamic_update_slice_in_dim(
        jnp.zeros(tokens.shape, jnp.bfloat16), result_rows, offset, 0
    )
    returned_pad = jnp.concatenate(
        [returned, jnp.zeros((tokens.shape[0] - SEND, local_cols), jnp.bfloat16)], axis=0
    )
    mixed_rows = jnp.where(row_ids < offset, returned_pad, placed)
    live_rows = (row_image < IMAGES)[:, None]
    mixed_rows = jnp.where(live_rows, mixed_rows, jnp.zeros_like(mixed_rows))
    member = row_image[None, :] == jnp.arange(IMAGES, dtype=jnp.int32)[:, None]
    pooled_sums = jnp.dot(
        member.astype(jnp.bfloat16), mixed_rows, preferred_element_type=jnp.float32
    )
    image_counts = jnp.sum(member.astype(jnp.float32), axis=1)
    pooled_sums, image_counts = lax.psum((pooled_sums, image_counts), "dp")
    return (mixed_rows, pooled_sums / image_counts[:, None])


def solution(mesh):
    return jax.shard_map(
        body,
        mesh=mesh,
        in_specs=(
            P(("groups", "dp"), "mp"),
            P(("groups", "dp")),
            P("mp"),
            P(("dp", "mp"), None),
            P(("dp", "mp")),
            P(("dp", "mp"), None),
            P("mp"),
        ),
        out_specs=(P(("groups", "dp"), "mp"), P("groups", "mp")),
        check_vma=False,
    )
```

profile of v0, /device:TPU:0, one launch (start us, length us, event | category | flops | bytes accessed | tf_op | source)
XLA Modules:
  0.0 809.7 jit_solution(8430670093058059554)
XLA Ops:
  7.2 0.0 all-gather.5.cloned.1.call-start
  7.2 0.8 slice.14
  8.0 0.5 collective-permute-start
  8.5 1.3 slice.12
  10.4 0.9 constant_dynamic-slice_fusion
  11.3 0.7 convert_element_type.26
  12.0 0.0 collective-permute-done
  12.0 0.8 slice_select_fusion
  12.8 0.2 convert_reduce_fusion
  13.0 22.6 %all-reduce.1 = (f32[160]{0:T(256)S(1)}, f32[160]{0:T(256)S(1)}) all-reduce(f32[160]{0:T(256)S(1)} %get-tuple-element.3, f32[160]{0:T(256)S(1)} %get-tuple-element.2), channel_id=1, replica_groups=mesh['groups'=2,'dp'=2,'mp'=8] {'mp'}, use_global_device_ids=true, to_apply=%region_3.4 | all-reduce | flops 320 | bytes 2560 | tf_op jit(solution)/shard_map/psum | solution.py:29
  35.7 0.9 fusion.45
  36.5 0.0 all-gather.5.cloned.1.call-update
  36.6 0.0 all-gather.9.cloned.1.call-start
  36.6 0.7 all-gather.9.cloned.1.call-update
  37.3 0.0 all-gather.7.cloned.1.call-start
  37.4 24.6 %copy.14 = bf16[384,24576]{0,1:T(8,128)(2,1)} copy(bf16[384,24576]{1,0:T(8,128)(2,1)} %param.10) | data formatting | bytes 37748736 | tf_op args[3]
  62.0 10.4 %copy.15 = bf16[384,2,8,1536]{0,3,1,2:T(8,128)(2,1)S(1)} copy(bf16[384,2,8,1536]{0,3,2,1:T(8,128)(2,1)} %bitcast.18) | data formatting | bytes 37748736 | tf_op jit(solution)/shard_map/reshape | solution.py:40
  72.4 413.9 %all_to_all.15 = bf16[384,2,8,1536]{0,3,1,2:T(8,128)(2,1)S(1)} all-to-all(bf16[384,2,8,1536]{0,3,1,2:T(8,128)(2,1)S(1)} %copy.15), channel_id=1, replica_groups=mesh['groups'=2,'dp'=2,'mp'=8] {'mp'}, dimensions={2} | all-to-all | bytes 37748736 | tf_op jit(solution)/shard_map/all_to_all | solution.py:43
  486.3 60.3 %copy.16 = bf16[8,384,2,1,1536]{1,0,4,2,3:T(8,128)(2,1)S(1)} copy(bf16[8,384,2,1,1536]{1,4,2,0,3:T(8,128)(2,1)S(1)} %bitcast.16) | data formatting | bytes 37748736 | tf_op jit(solution)/shard_map/all_to_all | solution.py:43
  546.6 8.5 %copy.17 = bf16[384,8,8,384]{3,1,2,0:T(8,128)(2,1)} copy(bf16[384,8,8,384]{3,2,1,0:T(8,128)(2,1)S(1)} %bitcast.17) | data formatting | bytes 37748736
  555.0 0.0 copy-start.1
  555.0 0.0 all-gather.7.cloned.1.call-update
  555.1 0.0 all-reduce.5.cloned.1.call-start
  555.1 0.6 copy-done.1
  555.7 1.8 all-gather
  557.5 0.0 all-gather.5.cloned.1.call-done
  557.6 0.0 all-gather.9.cloned.1.call-done
  557.6 53.6 %all-gather.7.cloned.1.call-done = bf16[6144,3072]{0,1:T(8,128)(2,1)} async-done(((bf16[3072,3072]{0,1:T(8,128)(2,1)}), bf16[6144,3072]{0,1:T(8,128)(2,1)}) %all-gather.7.cloned.1.call-update) | async-done | bytes 37748752 | tf_op jit(solution)/shard_map/all_gather | solution.py:47
  611.2 34.2 %fusion.10 = f32[160,6144]{1,0:T(8,128)} fusion(bf16[3072,6144]{1,0:T(8,128)(2,1)} %all-gather.9.cloned.1.call-done, bf16[160,6144]{1,0:T(8,128)(2,1)} %all-gather.5.cloned.1.call-done, bf16[6144,3072]{0,1:T(8,128)(2,1)} %all-gather.7.cloned.1.call-done, f32[3072]{0:T(1024)S(1)} %bitcast.19), kind=kOutput, calls=%fused_computation.20 | convolution fusion | flops 12112035840 | bytes 81408000 | tf_op jit(solution)/shard_map/dot_general | solution.py:57
  645.4 0.0 copy-start.2
  645.4 0.0 copy-start.3
  645.4 0.0 all-reduce.5.cloned.1.call-update
  645.5 0.6 copy-done.2
  646.1 0.0 copy-done.3
  646.1 0.1 convert_reduce_fusion.1
  646.2 149.9 %all-reduce.5.cloned.1.call-done = f32[160,6144]{1,0:T(8,128)} async-done(((f32[160,6144]{1,0:T(8,128)}), f32[160,6144]{1,0:T(8,128)}) %all-reduce.5.cloned.1.call-update) | async-done | bytes 3932176 | tf_op jit(solution)/shard_map/psum | solution.py:58
  796.2 1.1 constant_dynamic-update-slice_fusion
  797.3 0.1 collective-permute-start.1
  797.4 1.2 collective-permute-done.1
  798.6 0.2 select_select_fusion
  798.7 0.0 copy-start
  798.8 0.2 fusion.49
  798.9 3.6 all-reduce.2
  802.5 0.7 broadcast_divide_fusion
  803.2 0.0 copy-done
  (8 shorter events, 0.1 us)
Async XLA Ops:
  7.2 550.4 %all-gather.5.cloned.1.call-start = ((), (), s32[]{:S(2)}) async-start(), calls=%async_computation.1 | async-start | bytes 2211840 | tf_op jit(solution)/shard_map/all_gather | solution.py:37
  8.0 4.0 collective-permute-start
  36.6 521.0 %all-gather.9.cloned.1.call-start = ((), (), s32[]{:S(2)}) async-start(), calls=%async_computation.3 | async-start | bytes 56623104 | tf_op jit(solution)/shard_map/all_gather | solution.py:51
  37.3 573.9 %all-gather.7.cloned.1.call-start = ((), (), s32[]{:S(2)}) async-start(), calls=%async_computation.2 | async-start | bytes 56623104 | tf_op jit(solution)/shard_map/all_gather | solution.py:47
  555.0 0.7 copy-start.1
  555.1 241.1 %all-reduce.5.cloned.1.call-start = ((), (), s32[]{:S(2)}) async-start(), calls=%async_computation.4 | async-start | bytes 7864320 | tf_op jit(solution)/shard_map/psum | solution.py:58
  645.4 0.7 copy-start.2
  645.4 0.7 copy-start.3
  797.3 1.3 collective-permute-start.1
  798.7 4.4 copy-start
Sparse Core Ops, SparseCore 0:
  36.7 52.8 all-gather.4
  91.1 56.0 all-gather.8
  555.2 55.9 all-gather.6
  645.6 150.5 all-reduce.4
where the time goes:
time: 811 us; the launch traced here: 810 us
  blocking collectives  442 us (55%)
  waiting for transfers between devices  205 us (25%)
  local copies, waits for them, and re-layouts  108 us (13%)
  matrix products  34.4 us (4%)
  between operations  14.5 us (2%)
    all_to_all x1, blocking collectives, body(): lax.all_to_all(weight_blocks, 'mp', split_axis=2, concat_axis=0, tiled=True)  414 us
    psum x1, waiting for transfers between devices, body(): summed = lax.psum(partial_out, 'mp')  150 us
    all_to_all x1, local copies, waits for them, and re-layouts, body(): lax.all_to_all(weight_blocks, 'mp', split_axis=2, concat_axis=0, tiled=True)  60.3 us
    all_gather x1, waiting for transfers between devices, body(): lax.all_gather(relaid_rows, 'dp', axis=0, tiled=True)  53.6 us
    unnamed x11, local copies, waits for them, and re-layouts  34.4 us
    dot_general x1, matrix products, body(): partial_out = jnp.dot(hidden, down_rows, preferred_element_type=jnp.float32)  34.2 us
    psum x1, blocking collectives, body(): lax.psum((jnp.sum(work_values, axis=1), jnp.sum(work_values * work_values...  22.6 us
  transfers between devices with their start and end apart: 6, of which 3 were waited for; matrix products, arithmetic and copies ran while one was open for 13% of the time, Pallas kernels for 0%

commit v1 on v0

v1 whole, which is shorter than its diff:
```python
import jax
import jax.numpy as jnp
from jax import lax
from jax.sharding import PartitionSpec as P

SEND = 32
KEEP = 160
IMAGES = 10
EPSILON = 1e-06
PAIR = [(0, 1), (1, 0)]


def swap_dp(array):
    return lax.ppermute(array, "dp", PAIR)


def finish(row_image, offset, work_values, branch_out, outer_bias):
    rows, cols = row_image.shape[0], work_values.shape[1]
    result_rows = (work_values + branch_out + outer_bias.astype(jnp.float32)).astype(jnp.bfloat16)
    returned = swap_dp(result_rows[KEEP - SEND :])
    row_ids = jnp.arange(rows, dtype=jnp.int32)[:, None]
    placed = lax.dynamic_update_slice_in_dim(
        jnp.zeros((rows, cols), jnp.bfloat16), result_rows, offset, 0
    )
    returned_pad = jnp.concatenate(
        [returned, jnp.zeros((rows - SEND, cols), jnp.bfloat16)], axis=0
    )
    mixed_rows = jnp.where(row_ids < offset, returned_pad, placed)
    live_rows = (row_image < IMAGES)[:, None]
    mixed_rows = jnp.where(live_rows, mixed_rows, jnp.zeros_like(mixed_rows))
    member = row_image[None, :] == jnp.arange(IMAGES, dtype=jnp.int32)[:, None]
    pooled_sums = jnp.dot(
        member.astype(jnp.bfloat16), mixed_rows, preferred_element_type=jnp.float32
    )
    image_counts = jnp.sum(member.astype(jnp.float32), axis=1)
    pooled_sums, image_counts = lax.psum((pooled_sums, image_counts), "dp")
    return mixed_rows, pooled_sums / image_counts[:, None]


def general(tokens, row_image, norm_gain, inner_weight, inner_bias, outer_weight, outer_bias):
    width = inner_weight.shape[0] * lax.axis_size("dp") * lax.axis_size("mp")
    offset = jnp.where(row_image[KEEP] < IMAGES, SEND, 0).astype(jnp.int32)
    incoming = swap_dp(tokens[:SEND])
    own_rows = lax.dynamic_slice_in_dim(tokens, offset, KEEP - SEND, 0)
    tail_rows = jnp.where(offset > 0, tokens[KEEP:], incoming)
    work_values = jnp.concatenate([own_rows, tail_rows], axis=0).astype(jnp.float32)
    moments = lax.psum(
        (jnp.sum(work_values, axis=1), jnp.sum(work_values * work_values, axis=1)), "mp"
    )
    row_mean = (moments[0] / width)[:, None]
    row_var = (moments[1] / width)[:, None] - row_mean * row_mean
    own_normed = (
        (work_values - row_mean) * lax.rsqrt(row_var + EPSILON) * norm_gain.astype(jnp.float32)
    ).astype(jnp.bfloat16)
    normed = lax.all_gather(own_normed, "mp", axis=1, tiled=True)
    normed = lax.all_gather(normed, "dp", axis=0, tiled=True)
    slab = lax.axis_index("dp") * lax.axis_size("mp") + lax.axis_index("mp")
    features = inner_weight.shape[0]
    normed = lax.dynamic_slice_in_dim(normed, slab * features, features, 1)
    pre_act = jnp.dot(normed, inner_weight, preferred_element_type=jnp.float32)
    pre_act = lax.psum_scatter(pre_act, "dp", scatter_dimension=1, tiled=True)
    pre_act = lax.psum_scatter(pre_act, "mp", scatter_dimension=1, tiled=True)
    hidden = jax.nn.gelu(pre_act + inner_bias.astype(jnp.float32), approximate=False).astype(
        jnp.bfloat16
    )
    branch_out = jnp.dot(hidden, outer_weight, preferred_element_type=jnp.float32)
    branch_out = lax.psum_scatter(branch_out, "dp", scatter_dimension=0, tiled=True)
    branch_out = lax.psum_scatter(branch_out, "mp", scatter_dimension=1, tiled=True)
    return finish(row_image, offset, work_values, branch_out, outer_bias)


def solution(mesh):
    return jax.shard_map(
        general,
        mesh=mesh,
        in_specs=(
            P(("groups", "dp"), "mp"),
            P(("groups", "dp")),
            P("mp"),
            P(("dp", "mp"), None),
            P(("dp", "mp")),
            P(("dp", "mp"), None),
            P("mp"),
        ),
        out_specs=(P(("groups", "dp"), "mp"), P("groups", "mp")),
        check_vma=False,
    )
```

time: 811 us -> 554 us (0.68)
  blocking collectives: 442 us -> 26.2 us
  waiting for transfers between devices: 205 us -> 464 us
  local copies, waits for them, and re-layouts: 108 us -> 4.14 us
    all_to_all x1 -> x0, blocking collectives: 414 us -> none  [body(): lax.all_to_all(weight_blocks, 'mp', split_axis=2, concat_axis=0, tiled=True)]
    reduce_scatter x0 -> x4, waiting for transfers between devices: none -> 403 us  [the longest x1 255 us: general(): pre_act = lax.psum_scatter(pre_act, 'mp', scatter_dimension=1, tiled=True)]
    psum x1 -> x0, waiting for transfers between devices: 150 us -> none  [body(): summed = lax.psum(partial_out, 'mp')]
    all_to_all x1 -> x0, local copies, waits for them, and re-layouts: 60.3 us -> none  [body(): lax.all_to_all(weight_blocks, 'mp', split_axis=2, concat_axis=0, tiled=True)]
    unnamed x11 -> x8, local copies, waits for them, and re-layouts: 34.4 us -> 1.11 us
    reshape x1 -> x0, local copies, waits for them, and re-layouts: 10.4 us -> none  [body(): inner_weight.reshape(local_weight_rows, data_parts, model_parts, unit_cou...]
    all_gather x3 -> x2, waiting for transfers between devices: 53.6 us -> 59 us  [the longest x1 45.8 us: general(): normed = lax.all_gather(own_normed, 'mp', axis=1, tiled=True)]
    dot_general x2 -> x3, matrix products: 34.4 us -> 38.6 us  [the longest x1 20.2 us: general(): jnp.dot(hidden, outer_weight, preferred_element_type=jnp.float32)]
  transfers between devices with their start and end apart: 6 -> 8, of which waited for: 3 -> 7; matrix products, arithmetic and copies ran while one was open for 13% -> 1% of each run, Pallas kernels for 0% -> 0%
where the time goes in v1:
time: 554 us; the launch traced here: 553 us
  waiting for transfers between devices  464 us (84%)
  matrix products  38.6 us (7%)
  blocking collectives  26.2 us (5%)
  between operations  14.8 us (3%)
    reduce_scatter x1, waiting for transfers between devices, general(): pre_act = lax.psum_scatter(pre_act, 'mp', scatter_dimension=1, tiled=True)  255 us
    reduce_scatter x1, waiting for transfers between devices, general(): lax.psum_scatter(branch_out, 'mp', scatter_dimension=1, tiled=True)  88.7 us
    all_gather x1, waiting for transfers between devices, general(): normed = lax.all_gather(own_normed, 'mp', axis=1, tiled=True)  45.8 us
    reduce_scatter x1, waiting for transfers between devices, general(): pre_act = lax.psum_scatter(pre_act, 'dp', scatter_dimension=1, tiled=True)  44 us
    psum x1, blocking collectives, general(): lax.psum((jnp.sum(work_values, axis=1), jnp.sum(work_values * work_values...  22.6 us
    dot_general x1, matrix products, general(): jnp.dot(hidden, outer_weight, preferred_element_type=jnp.float32)  20.2 us
    dot_general x1, matrix products, general(): pre_act = jnp.dot(normed, inner_weight, preferred_element_type=jnp.float32)  18.3 us
    reduce_scatter x1, waiting for transfers between devices, general(): lax.psum_scatter(branch_out, 'dp', scatter_dimension=0, tiled=True)  15.7 us
  transfers between devices with their start and end apart: 8, of which 7 were waited for; matrix products, arithmetic and copies ran while one was open for 1% of the time, Pallas kernels for 0%

profile of v1, /device:TPU:0, one launch (start us, length us, event | category | flops | bytes accessed | tf_op | source)
XLA Modules:
  0.0 553.2 jit_solution(5498175911741584731)
XLA Ops:
  7.2 0.0 all-gather.3.cloned.1.call-start
  7.2 0.8 slice.14
  8.0 0.5 collective-permute-start
  8.5 1.3 slice.12
  10.4 0.9 constant_dynamic-slice_fusion
  11.3 0.7 convert_element_type.26
  12.0 0.0 collective-permute-done
  12.0 0.8 slice_select_fusion
  12.8 0.2 convert_reduce_fusion
  13.0 22.6 %all-reduce.1 = (f32[160]{0:T(256)S(1)}, f32[160]{0:T(256)S(1)}) all-reduce(f32[160]{0:T(256)S(1)} %get-tuple-element.3, f32[160]{0:T(256)S(1)} %get-tuple-element.2), channel_id=1, replica_groups=mesh['groups'=2,'dp'=2,'mp'=8] {'mp'}, use_global_device_ids=true, to_apply=%region_3.4 | all-reduce | flops 320 | bytes 2560 | tf_op jit(solution)/shard_map/psum | solution.py:47
  35.7 0.9 fusion.45
  36.5 0.0 all-gather.3.cloned.1.call-update
  36.6 0.0 all-gather.5.cloned.1.call-start
  36.6 45.8 %all-gather.3.cloned.1.call-done = bf16[160,6144]{1,0:T(8,128)(2,1)} async-done(((bf16[160,768]{1,0:T(8,128)(2,1)}), bf16[160,6144]{1,0:T(8,128)(2,1)}) %all-gather.3.cloned.1.call-update) | async-done | bytes 1966096 | tf_op jit(solution)/shard_map/all_gather | solution.py:55
  82.4 0.0 all-gather.5.cloned.1.call-update
  82.4 0.0 reduce-scatter.5.cloned.1.call-start
  82.5 13.2 %all-gather.5.cloned.1.call-done = bf16[320,6144]{1,0:T(8,128)(2,1)} async-done(((bf16[160,6144]{1,0:T(8,128)(2,1)}), bf16[320,6144]{1,0:T(8,128)(2,1)}) %all-gather.5.cloned.1.call-update) | async-done | bytes 3932176 | tf_op jit(solution)/shard_map/all_gather | solution.py:56
  95.7 18.3 %fusion.49 = f32[320,24576]{1,0:T(8,128)} fusion(bf16[384,24576]{1,0:T(8,128)(2,1)} %param.10, bf16[320,6144]{1,0:T(8,128)(2,1)} %all-gather.5.cloned.1.call-done, s32[]{:T(128)S(6)} %select_n.31), kind=kOutput, calls=%fused_computation.63 | convolution fusion | flops 6039797760 | bytes 50577412 | tf_op jit(solution)/shard_map/dot_general | solution.py:60
  114.0 0.0 reduce-scatter.5.cloned.1.call-update
  114.0 0.0 reduce-scatter.7.cloned.1.call-start
  114.0 44.0 %reduce-scatter.5.cloned.1.call-done = f32[320,12288]{1,0:T(8,128)} async-done(((f32[320,24576]{1,0:T(8,128)}), f32[320,12288]{1,0:T(8,128)}) %reduce-scatter.5.cloned.1.call-update) | async-done | bytes 15728656 | tf_op jit(solution)/shard_map/reduce_scatter | solution.py:61
  158.0 0.0 copy-start.1
  158.0 0.0 reduce-scatter.7.cloned.1.call-update
  158.0 0.2 reduce-scatter.9.cloned.1.call-start
  158.3 0.4 copy-done.1
  158.7 255.1 %reduce-scatter.7.cloned.1.call-done = f32[320,1536]{1,0:T(8,128)} async-done(((f32[320,12288]{1,0:T(8,128)}), f32[320,1536]{1,0:T(8,128)}) %reduce-scatter.7.cloned.1.call-update) | async-done | bytes 1966096 | tf_op jit(solution)/shard_map/reduce_scatter | solution.py:62
  413.8 20.2 %fusion.10 = f32[320,6144]{1,0:T(8,128)} fusion(bf16[1536,6144]{1,0:T(8,128)(2,1)} %param.12, f32[320,1536]{1,0:T(8,128)} %reduce-scatter.7.cloned.1.call-done, f32[1536]{0:T(1024)S(1)} %convert_element_type.28), kind=kOutput, calls=%fused_computation.19 | convolution fusion | flops 6072238080 | bytes 28710912 | tf_op jit(solution)/shard_map/dot_general | solution.py:66
  434.0 0.0 reduce-scatter.9.cloned.1.call-update
  434.0 0.0 reduce-scatter.11.cloned.1.call-start
  434.0 15.7 %reduce-scatter.9.cloned.1.call-done = f32[160,6144]{1,0:T(8,128)} async-done(((f32[320,6144]{1,0:T(8,128)}), f32[160,6144]{1,0:T(8,128)}) %reduce-scatter.9.cloned.1.call-update) | async-done | bytes 3932176 | tf_op jit(solution)/shard_map/reduce_scatter | solution.py:67
  449.7 0.0 copy-start.2
  449.7 0.0 copy-start.3
  449.7 0.0 reduce-scatter.11.cloned.1.call-update
  449.8 0.7 copy-done.2
  450.4 0.0 copy-done.3
  450.4 0.1 convert_reduce_fusion.1
  450.6 88.7 %reduce-scatter.11.cloned.1.call-done = f32[160,768]{1,0:T(8,128)} async-done(((f32[160,6144]{1,0:T(8,128)}), f32[160,768]{1,0:T(8,128)}) %reduce-scatter.11.cloned.1.call-update) | async-done | bytes 491536 | tf_op jit(solution)/shard_map/reduce_scatter | solution.py:68
  539.3 1.1 constant_dynamic-update-slice_fusion
  540.4 0.1 collective-permute-start.1
  540.5 1.2 collective-permute-done.1
  541.7 0.2 select_select_fusion
  541.9 0.0 copy-start
  541.9 0.2 fusion.51
  542.0 3.6 all-reduce.2
  545.6 0.7 broadcast_divide_fusion
  546.3 0.0 copy-done
  (7 shorter events, 0.1 us)
Async XLA Ops:
  7.2 75.2 %all-gather.3.cloned.1.call-start = ((), (), s32[]{:S(2)}) async-start(), calls=%async_computation.4 | async-start | bytes 2211840 | tf_op jit(solution)/shard_map/all_gather | solution.py:55
  8.0 4.0 collective-permute-start
  36.6 59.1 %all-gather.5.cloned.1.call-start = ((), (), s32[]{:S(2)}) async-start(), calls=%async_computation.5 | async-start | bytes 5898240 | tf_op jit(solution)/shard_map/all_gather | solution.py:56
  82.4 75.6 %reduce-scatter.5.cloned.1.call-start = ((), (), s32[]{:S(2)}) async-start(), calls=%async_computation.6 | async-start | bytes 47185920 | tf_op jit(solution)/shard_map/reduce_scatter | solution.py:61
  114.0 299.8 %reduce-scatter.7.cloned.1.call-start = ((), (), s32[]{:S(2)}) async-start(), calls=%async_computation.7 | async-start | bytes 17694720 | tf_op jit(solution)/shard_map/reduce_scatter | solution.py:62
  158.0 0.7 copy-start.1
  158.0 291.7 %reduce-scatter.9.cloned.1.call-start = ((), (), s32[]{:S(2)}) async-start(), calls=%async_computation.8 | async-start | bytes 11796480 | tf_op jit(solution)/shard_map/reduce_scatter | solution.py:67
  434.0 105.3 %reduce-scatter.11.cloned.1.call-start = ((), (), s32[]{:S(2)}) async-start(), calls=%async_computation.9 | async-start | bytes 4423680 | tf_op jit(solution)/shard_map/reduce_scatter | solution.py:68
  449.7 0.7 copy-start.2
  449.7 0.7 copy-start.3
  540.4 1.3 collective-permute-start.1
  541.9 4.4 copy-start
Sparse Core Ops, SparseCore 0:
  36.7 45.6 all-gather.2
  83.9 11.7 all-gather.4
  114.1 43.8 reduce-scatter.4
  161.5 252.2 reduce-scatter.6
  434.1 15.5 reduce-scatter.8
  453.7 85.4 reduce-scatter.10

commit v2 on v1

--- a/solution.py
+++ b/solution.py
@@ -7,6 +7,7 @@
 KEEP = 160
 IMAGES = 10
 EPSILON = 1e-06
+PARTS = 1
 PAIR = [(0, 1), (1, 0)]
 
 
@@ -69,9 +70,210 @@
     return finish(row_image, offset, work_values, branch_out, outer_bias)
 
 
+ACROSS = [(i, i ^ 1) for i in range(8)]
+ORDER = ((3, 2, 1, 0), (3, 2, 0, 1), (0, 1, 3, 2), (0, 1, 2, 3))
+DEPTH = 2
+
+
+def along_z(*moves):
+    return [(2 * a + x, 2 * b + x) for a, b in moves for x in (0, 1)]
+
+
+ENDS_IN = along_z((0, 1), (3, 2))
+UP_TWO = along_z((0, 1), (1, 2))
+DOWN_TWO = along_z((3, 2), (2, 1))
+UP_ALL = along_z((0, 1), (1, 2), (2, 3))
+DOWN_ALL = along_z((3, 2), (2, 1), (1, 0))
+
+
+def shift(array, moves):
+    return lax.ppermute(array.astype(jnp.bfloat16), "mp", moves).astype(jnp.float32)
+
+
+def after(array, other):
+    return lax.optimization_barrier((array, other))[0]
+
+
+class Across:
+    def __init__(self):
+        self.done = []
+
+    def send(self, array):
+        array = array.astype(jnp.bfloat16)
+        if len(self.done) >= DEPTH:
+            array = after(array, self.done[-DEPTH])
+        self.done.append(lax.ppermute(array, "mp", ACROSS))
+        return self.done[-1].astype(jnp.float32)
+
+
+class Scatter:
+    def __init__(self, across, block, z):
+        self.across, self.block, self.z = across, block, z
+        self.kept = []
+
+    def step(self):
+        step, z, kept = len(self.kept), self.z, self.kept
+        sent, own = self.block(step)
+        kept.append(own + self.across.send(sent))
+        if step == 0:
+            self.first = shift(kept[0], ENDS_IN)
+        elif step == 1:
+            ends = (z == 0) | (z == 3)
+            second = jnp.where(ends, kept[1], kept[0] + self.first).astype(jnp.bfloat16)
+            self.up, self.down = shift(second, UP_TWO), shift(second, DOWN_TWO)
+        elif step == 2:
+            up = jnp.where(z == 1, kept[1], kept[2]) + self.up
+            down = jnp.where(z == 2, kept[1], kept[2]) + self.down
+            self.up, self.down = shift(up, UP_ALL), shift(down, DOWN_ALL)
+        else:
+            return kept[3] + self.up + self.down
+
+
+def eight(tokens, row_image, norm_gain, inner_weight, inner_bias, outer_weight, outer_bias):
+    shard_rows, cols = tokens.shape
+    features, units = inner_weight.shape
+    half = cols // 2
+    width = cols * 8
+    dp, mp = lax.axis_index("dp"), lax.axis_index("mp")
+    x, z = lax.rem(mp, 2), mp // 2
+    order = jnp.asarray(ORDER, jnp.int32)[z]
+    loaded = row_image[KEEP] < IMAGES
+
+    sheet = jnp.concatenate([tokens, jnp.broadcast_to(norm_gain[None, :], (16, cols))], axis=0)
+    upper = mp // 4
+    same = lax.dynamic_slice_in_dim(sheet, upper * half, half, 1)
+    other = lax.dynamic_slice_in_dim(sheet, (1 - upper) * half, half, 1)
+    same = lax.ppermute(same, "mp", [(4 * e + q, 2 * q + e) for e in (0, 1) for q in range(4)])
+    other = lax.ppermute(other, "mp", [(4 * e + q, 2 * q + 1 - e) for e in (0, 1) for q in range(4)])
+
+    values = tokens.astype(jnp.float32)
+    moments = jnp.stack([jnp.sum(values, axis=1), jnp.sum(values * values, axis=1)])
+    moments = moments + lax.ppermute(moments, "mp", [(i, i ^ 1) for i in range(8)])
+    inner_weight = after(inner_weight, moments)
+    for bit in (2, 4):
+        moments = moments + lax.ppermute(moments, "mp", [(i, i ^ bit) for i in range(8)])
+    row_mean = (moments[0] / width)[:, None]
+    row_var = (moments[1] / width)[:, None] - row_mean * row_mean
+    scale = lax.rsqrt(row_var + EPSILON)
+
+    low_first = x == dp
+    slab = jnp.where(
+        low_first,
+        jnp.concatenate([same, other], axis=1),
+        jnp.concatenate([other, same], axis=1),
+    ).astype(jnp.float32)
+    own = ((slab[:shard_rows] - row_mean) * scale * slab[shard_rows : shard_rows + 1]).astype(
+        jnp.bfloat16
+    )
+    theirs = swap_dp(own)
+    theirs = jnp.concatenate([theirs[:, half:], theirs[:, :half]], axis=1)
+    my_work = jnp.where(
+        loaded, own[SEND:], jnp.concatenate([own[: KEEP - SEND], theirs[:SEND]], axis=0)
+    )
+    their_work = jnp.where(
+        loaded, jnp.concatenate([theirs[: KEEP - SEND], own[:SEND]], axis=0), theirs[SEND:]
+    )
+    edges = [(i * KEEP // PARTS, (i + 1) * KEEP // PARTS) for i in range(PARTS)]
+    parts = [
+        lax.optimization_barrier(jnp.concatenate([my_work[a:b], their_work[a:b]], axis=0))
+        for a, b in edges
+    ]
+
+    pair = units // 8
+    one = pair // 2
+    lent = []
+    for step in range(4):
+        start = (1 - dp) * (units // 2) + order[step] * pair
+        lent.append(swap_dp(lax.dynamic_slice_in_dim(inner_weight, start, pair, 1)))
+
+    def inner_block(rows):
+        def block(step):
+            def product(side):
+                mine = lax.dynamic_slice_in_dim(
+                    inner_weight, dp * (units // 2) + order[step] * pair + side * one, one, 1
+                )
+                got = lax.dynamic_slice_in_dim(lent[step], side * one, one, 1)
+                return jnp.dot(
+                    rows[:, :features], mine, preferred_element_type=jnp.float32
+                ) + jnp.dot(rows[:, features:], got, preferred_element_type=jnp.float32)
+
+            return product(1 - x), product(x)
+
+        return block
+
+    def outer_block(hidden):
+        mine = hidden.shape[0] // 2
+
+        def block(step):
+            def product(side):
+                start = order[step] * 2 * cols + side * cols
+                weight = lax.dynamic_slice_in_dim(outer_weight, start, cols, 1)
+                out = jnp.dot(hidden, weight, preferred_element_type=jnp.float32)
+                return out[:mine] + swap_dp(out[mine:])
+
+            return product(1 - x), product(x)
+
+        return block
+
+    def activate(pre_act):
+        hidden = jax.nn.gelu(pre_act + inner_bias.astype(jnp.float32), approximate=False)
+        return lax.optimization_barrier(hidden.astype(jnp.bfloat16))
+
+    across = Across()
+    inner = [Scatter(across, inner_block(rows), z) for rows in parts]
+    outer, branch_out = [], []
+    for i in range(PARTS):
+        for step in range(4):
+            pre_act = inner[i].step()
+            if i and step > 1:
+                branch_out.append(outer[-1].step())
+                if step == 3:
+                    branch_out.append(outer[-1].step())
+            elif i and step == 1:
+                outer[-1].step()
+        outer.append(Scatter(across, outer_block(activate(pre_act)), z))
+    for step in range(4):
+        branch_out.append(outer[-1].step())
+    branch_out = jnp.concatenate([part for part in branch_out if part is not None], axis=0)
+
+    their_image = swap_dp(row_image)
+    incoming = swap_dp(tokens[:SEND])
+    work_tokens = jnp.where(
+        loaded, tokens[SEND:], jnp.concatenate([tokens[: KEEP - SEND], incoming], axis=0)
+    )
+    work_image = jnp.where(
+        loaded,
+        row_image[SEND:],
+        jnp.concatenate([row_image[: KEEP - SEND], their_image[:SEND]], axis=0),
+    )
+    result = (
+        work_tokens.astype(jnp.float32) + branch_out + outer_bias.astype(jnp.float32)
+    ).astype(jnp.bfloat16)
+    result = jnp.where((work_image < IMAGES)[:, None], result, jnp.zeros_like(result))
+    images = jnp.arange(IMAGES, dtype=jnp.int32)[:, None]
+    sums = jnp.dot(
+        (work_image[None, :] == images).astype(jnp.bfloat16),
+        result,
+        preferred_element_type=jnp.float32,
+    )
+    counts = jnp.sum((row_image[None, :] == images).astype(jnp.float32), axis=1) + jnp.sum(
+        (their_image[None, :] == images).astype(jnp.float32), axis=1
+    )
+    returned = swap_dp(result[KEEP - SEND :])
+    sums = sums + swap_dp(sums)
+    mixed_rows = jnp.where(
+        loaded,
+        jnp.concatenate([returned, result], axis=0),
+        jnp.concatenate(
+            [result[: KEEP - SEND], jnp.zeros((shard_rows - KEEP + SEND, cols), jnp.bfloat16)], axis=0
+        ),
+    )
+    return mixed_rows, sums / counts[:, None]
+
+
 def solution(mesh):
     return jax.shard_map(
-        general,
+        eight if mesh.shape["mp"] == 8 and mesh.shape["dp"] == 2 else general,
         mesh=mesh,
         in_specs=(
             P(("groups", "dp"), "mp"),

time: 554 us -> 202 us (0.36)
  waiting for transfers between devices: 464 us -> 84.9 us
  starting transfers between devices: 0.94 us -> 48.7 us
  blocking collectives: 26.2 us -> 0 us
  between operations: 14.8 us -> 7.22 us
  local copies, waits for them, and re-layouts: 4.14 us -> 9.82 us
    reduce_scatter x4 -> x0, waiting for transfers between devices: 403 us -> none  [the longest x1 255 us: general(): pre_act = lax.psum_scatter(pre_act, 'mp', scatter_dimension=1, tiled=True)]
    ppermute x0 -> x23, waiting for transfers between devices: none -> 82 us  [the longest x8 47 us: send(): self.done.append(lax.ppermute(array, 'mp', ACROSS))]
    all_gather x2 -> x0, waiting for transfers between devices: 59 us -> none  [the longest x1 45.8 us: general(): normed = lax.all_gather(own_normed, 'mp', axis=1, tiled=True)]
    ppermute x0 -> x23, starting transfers between devices: none -> 45.7 us  [the longest x10 29.4 us: shift(): lax.ppermute(array.astype(jnp.bfloat16), 'mp', moves).astype(jnp.float32)]
    psum x2 -> x0, blocking collectives: 26.2 us -> none  [the longest x1 22.6 us: general(): lax.psum((jnp.sum(work_values, axis=1), jnp.sum(work_values * work_values...]
    dynamic_slice x1 -> x2, local copies, waits for them, and re-layouts: 0.94 us -> 7.47 us  [the longest x1 6.79 us: eight(): lent.append(swap_dp(lax.dynamic_slice_in_dim(inner_weight, start, pair, 1)))]
    dot_general x3 -> x25, matrix products: 38.6 us -> 43.9 us  [the longest x8 20.5 us: product(): jnp.dot(rows[:, features:], got, preferred_element_type=jnp.float32)]
  transfers between devices with their start and end apart: 8 -> 40, of which waited for: 7 -> 17; matrix products, arithmetic and copies ran while one was open for 1% -> 28% of each run, Pallas kernels for 0% -> 0%
where the time goes in v2:
time: 202 us; the launch traced here: 201 us
  waiting for transfers between devices  84.9 us (42%)
  starting transfers between devices  48.7 us (24%)
  matrix products  43.9 us (22%)
  local copies, waits for them, and re-layouts  9.82 us (5%)
  between operations  7.22 us (4%)
  other arithmetic  6.42 us (3%)
    ppermute x8, waiting for transfers between devices, send(): self.done.append(lax.ppermute(array, 'mp', ACROSS))  47 us
    ppermute x10, starting transfers between devices, shift(): lax.ppermute(array.astype(jnp.bfloat16), 'mp', moves).astype(jnp.float32)  29.4 us
    ppermute x10, waiting for transfers between devices, shift(): lax.ppermute(array.astype(jnp.bfloat16), 'mp', moves).astype(jnp.float32)  26.5 us
    dot_general x8, matrix products, product(): jnp.dot(rows[:, features:], got, preferred_element_type=jnp.float32)  20.5 us
    dot_general x8, matrix products, product(): jnp.dot(rows[:, :features], mine, preferred_element_type=jnp.float32)  15.6 us
    ppermute x1, waiting for transfers between devices, eight(): lax.ppermute(other, 'mp', [(4 * e + q, 2 * q + 1 - e) for e in (0, 1) for...  8.54 us
    dot_general x8, matrix products, product(): out = jnp.dot(hidden, weight, preferred_element_type=jnp.float32)  7.63 us
    dynamic_slice x1, local copies, waits for them, and re-layouts, eight(): lent.append(swap_dp(lax.dynamic_slice_in_dim(inner_weight, start, pair, 1)))  6.79 us
  transfers between devices with their start and end apart: 40, of which 17 were waited for; matrix products, arithmetic and copies ran while one was open for 28% of the time, Pallas kernels for 0%

profile of v2, /device:TPU:0, one launch (start us, length us, event | category | flops | bytes accessed | tf_op | source)
XLA Modules:
  0.0 200.9 jit_solution(3317058487209750714)
XLA Ops:
  0.6 1.2 convert_reduce_fusion
  1.8 3.0 %collective-permute-start.4 = (f32[2,192]{1,0:T(2,128)S(1)}, f32[2,192]{1,0:T(2,128)S(1)}, u32[]{:S(2)}, u32[]{:S(2)}) collective-permute-start(f32[2,192]{1,0:T(2,128)S(1)} %pad_maximum_fusion.3), channel_id=1, source_target_pairs={{0,1},{1,0},{2,3},{3,2},{4,5},{5,4},{6,7},{7,6},{8,9},{9,8},{10,11... | collective-permute-start | bytes 4616 | tf_op jit(solution)/shard_map/ppermute | solution.py:151
  8.7 1.6 collective-permute-start.5
  10.4 6.8 %constant_dynamic-slice_fusion.3 = (bf16[384,3072]{1,0:T(8,128)(2,1)S(1)}, bf16[384,3072]{1,0:T(8,128)(2,1)}, bf16[384,3072]{1,0:T(8,128)(2,1)}, bf16[384,3072]{1,0:T(8,128)(2,1)}) fusion(bf16[384,24576]{1,0:T(8,128)(2,1)} %param.11, s32[]{:T(128)S(6)} %select_n.188, s32[]{:T(128)S(6)} %select_n.200, s32[]{:T(128)S(6)} %select_n.197, s32[]{:T(128)S(6)} %select_n.193), kind=kLoop, calls=%fused_computation.182 | loop fusion | bytes 18874384 | tf_op jit(solution)/shard_map/dynamic_slice | solution.py:187
  17.2 2.7 %collective-permute-start.6 = (f32[2,192]{1,0:T(2,128)S(1)}, f32[2,192]{1,0:T(2,128)S(1)}, u32[]{:S(2)}, u32[]{:S(2)}) collective-permute-start(f32[2,192]{1,0:T(2,128)S(1)} %fusion.143), channel_id=1, source_target_pairs={{0,4},{1,5},{2,6},{3,7},{4,0},{5,1},{6,2},{7,3},{8,12},{9,13},{10,... | collective-permute-start | bytes 4616 | tf_op jit(solution)/shard_map/ppermute | solution.py:154
  20.6 3.2 %collective-permute-start.3 = (bf16[208,384]{1,0:T(8,128)(2,1)S(1)}, bf16[208,384]{1,0:T(8,128)(2,1)S(1)}, u32[]{:S(2)}, u32[]{:S(2)}) collective-permute-start(bf16[208,384]{1,0:T(8,128)(2,1)S(1)} %get-tuple-element.31), channel_id=1, source_target_pairs={{0,1},{1,3},{2,5},{3,7},{4,0},{5,2},{6,4},{7,6},{8,9},{9,11},{10,1... | collective-permute-start | bytes 479240 | tf_op jit(solution)/shard_map/ppermute | solution.py:147
  23.8 8.5 %collective-permute-done.3 = bf16[208,384]{1,0:T(8,128)(2,1)S(1)} collective-permute-done((bf16[208,384]{1,0:T(8,128)(2,1)S(1)}, bf16[208,384]{1,0:T(8,128)(2,1)S(1)}, u32[]{:S(2)}, u32[]{:S(2)}) %collective-permute-start.3) | collective-permute-done | bytes 159776 | tf_op jit(solution)/shard_map/ppermute | solution.py:147
  34.7 1.9 fusion.41
  36.7 2.9 %fusion.10 = bf16[320,1536]{1,0:T(8,128)(2,1)} fusion(f32[320,1536]{1,0:T(8,128)S(1)} %fusion.41, bf16[384,3072]{1,0:T(8,128)(2,1)} %collective-permute-done.13, s32[]{:T(128)S(6)} %select_n.191, bf16[320,768]{1,0:T(8,128)(2,1)S(1)} %pad_maximum_fusion), kind=kOutput, calls=%fused_computation.19 | convolution fusion | flops 378470400 | bytes 4374532 | tf_op jit(solution)/shard_map/dot_general | solution.py:198
  40.4 1.9 fusion.38
  42.3 1.9 fusion.53
  44.3 2.0 fusion.8
  46.3 1.3 collective-permute-start.10
  47.6 17.0 %collective-permute-done.14 = bf16[320,1536]{1,0:T(8,128)(2,1)} collective-permute-done((bf16[320,1536]{1,0:T(8,128)(2,1)}, bf16[320,1536]{1,0:T(8,128)(2,1)}, u32[]{:S(2)}, u32[]{:S(2)}) %collective-permute-start.14) | collective-permute-done | bytes 983072 | tf_op jit(solution)/shard_map/ppermute | solution.py:105
  64.5 2.2 %fusion.133 = (bf16[320,1536]{1,0:T(8,128)(2,1)S(1)}, f32[320,1536]{1,0:T(8,128)S(1)}) fusion(bf16[320,1536]{1,0:T(8,128)(2,1)} %collective-permute-done.14, f32[320,1536]{1,0:T(8,128)S(1)} %fusion.38, bf16[384,3072]{1,0:T(8,128)(2,1)} %collective-permute-done.13, s32[]{:T(128)S(6)} %select_n.189, bf16[320,768]{1,0:T(8,128)(2,1)S(1)} %pad_maximum_fusion), kind=kOutput, calls=%fused_computation.196 | convolution fusion | flops 379453440 | bytes 7323652 | tf_op jit(solution)/shard_map/dot_general | solution.py:198
  66.8 2.4 %collective-permute-start.16 = (bf16[320,1536]{1,0:T(8,128)(2,1)S(1)}, bf16[320,1536]{1,0:T(8,128)(2,1)S(1)}, u32[]{:S(2)}, u32[]{:S(2)}) collective-permute-start(bf16[320,1536]{1,0:T(8,128)(2,1)S(1)} %get-tuple-element.42), channel_id=1, source_target_pairs={{0,2},{1,3},{6,4},{7,5},{8,10},{9,11},{14,12},{15,13},{16,18},{17,... | collective-permute-start | bytes 2949128 | tf_op jit(solution)/shard_map/ppermute | solution.py:90
  69.2 1.9 fusion.44
  71.2 1.9 fusion.50
  73.1 2.0 fusion.9
  75.7 9.8 %collective-permute-done.10 = bf16[320,1536]{1,0:T(8,128)(2,1)S(1)} collective-permute-done((bf16[320,1536]{1,0:T(8,128)(2,1)S(1)}, bf16[320,1536]{1,0:T(8,128)(2,1)S(1)}, u32[]{:S(2)}, u32[]{:S(2)}) %collective-permute-start.10) | collective-permute-done | bytes 983072 | tf_op jit(solution)/shard_map/ppermute | solution.py:105
  85.5 2.0 fusion.2
  87.5 1.1 collective-permute-done.16
  89.1 4.4 %collective-permute-start.17 = (bf16[320,1536]{1,0:T(8,128)(2,1)S(1)}, bf16[320,1536]{1,0:T(8,128)(2,1)S(1)}, u32[]{:S(2)}, u32[]{:S(2)}) collective-permute-start(bf16[320,1536]{1,0:T(8,128)(2,1)S(1)} %select_convert_fusion), channel_id=1, source_target_pairs={{0,2},{1,3},{2,4},{3,5},{8,10},{9,11},{10,12},{11,13},{16,18},{17,... | collective-permute-start | bytes 2949128 | tf_op jit(solution)/shard_map/ppermute | solution.py:90
  94.3 1.9 fusion.47
  96.2 1.9 fusion.56
  100.2 6.4 %collective-permute-done.15 = bf16[320,1536]{1,0:T(8,128)(2,1)S(1)} collective-permute-done((bf16[320,1536]{1,0:T(8,128)(2,1)S(1)}, bf16[320,1536]{1,0:T(8,128)(2,1)S(1)}, u32[]{:S(2)}, u32[]{:S(2)}) %collective-permute-start.15) | collective-permute-done | bytes 983072 | tf_op jit(solution)/shard_map/ppermute | solution.py:105
  106.6 2.0 fusion.1
  108.6 3.4 %collective-permute-done.17 = bf16[320,1536]{1,0:T(8,128)(2,1)S(1)} collective-permute-done((bf16[320,1536]{1,0:T(8,128)(2,1)S(1)}, bf16[320,1536]{1,0:T(8,128)(2,1)S(1)}, u32[]{:S(2)}, u32[]{:S(2)}) %collective-permute-start.17) | collective-permute-done | bytes 983072 | tf_op jit(solution)/shard_map/ppermute | solution.py:90
  112.0 1.6 add_convert_fusion.1
  113.6 7.3 %collective-permute-start.18 = (bf16[320,1536]{1,0:T(8,128)(2,1)}, bf16[320,1536]{1,0:T(8,128)(2,1)}, u32[]{:S(2)}, u32[]{:S(2)}) collective-permute-start(bf16[320,1536]{1,0:T(8,128)(2,1)} %get-tuple-element.26), channel_id=1, source_target_pairs={{0,2},{1,3},{2,4},{3,5},{4,6},{5,7},{8,10},{9,11},{10,12},{11,13},... | collective-permute-start | bytes 2949128 | tf_op jit(solution)/shard_map/ppermute | solution.py:90
  120.9 1.5 collective-permute-start.20
  125.0 2.1 %fusion.59 = f32[320,1536]{1,0:T(8,128)S(1)} fusion(bf16[384,24576]{1,0:T(8,128)(2,1)} %param.11, s32[]{:T(128)S(6)} %select_n.187, bf16[320,768]{1,0:T(8,128)(2,1)S(1)} %pad_maximum_fusion), kind=kOutput, calls=%fused_computation.79 | convolution fusion | flops 377487360 | bytes 3391492 | tf_op jit(solution)/shard_map/dot_general | solution.py:196
  127.2 10.7 %collective-permute-done.18 = bf16[320,1536]{1,0:T(8,128)(2,1)} collective-permute-done((bf16[320,1536]{1,0:T(8,128)(2,1)}, bf16[320,1536]{1,0:T(8,128)(2,1)}, u32[]{:S(2)}, u32[]{:S(2)}) %collective-permute-start.18) | collective-permute-done | bytes 983072 | tf_op jit(solution)/shard_map/ppermute | solution.py:90
  137.9 4.9 %collective-permute-done.20 = bf16[320,1536]{1,0:T(8,128)(2,1)} collective-permute-done((bf16[320,1536]{1,0:T(8,128)(2,1)S(1)}, bf16[320,1536]{1,0:T(8,128)(2,1)}, u32[]{:S(2)}, u32[]{:S(2)}) %collective-permute-start.20) | collective-permute-done | bytes 983072 | tf_op jit(solution)/shard_map/ppermute | solution.py:90
  142.8 6.7 %fusion.29 = bf16[320,1536]{1,0:T(8,128)(2,1)S(1)} fusion(bf16[320,1536]{1,0:T(8,128)(2,1)} %collective-permute-done.20, bf16[320,1536]{1,0:T(8,128)(2,1)} %collective-permute-done.18, bf16[320,1536]{1,0:T(8,128)(2,1)} %collective-permute-done.11, f32[320,1536]{1,0:T(8,128)S(1)} %fusion.59, bf16[384,3072]{1,0:T(8,128)(2,1)S(1)} %copy-done.2, ...), kind=kOutput, calls=%fused_computation.38 | convolution fusion | flops 413368320 | bytes 7331844 | tf_op jit(solution)/shard_map/dot_general | solution.py:198
  155.8 1.0 fusion.19
  156.8 1.0 fusion.17
  159.6 1.2 collective-permute-done.32
  161.0 6.5 %collective-permute-done.30 = bf16[160,768]{1,0:T(8,128)(2,1)S(1)} collective-permute-done((bf16[160,768]{1,0:T(8,128)(2,1)S(1)}, bf16[160,768]{1,0:T(8,128)(2,1)S(1)}, u32[]{:S(2)}, u32[]{:S(2)}) %collective-permute-start.30) | collective-permute-done | bytes 245792 | tf_op jit(solution)/shard_map/ppermute | solution.py:105
  168.0 1.4 collective-permute-start.33
  169.5 5.5 %collective-permute-done.24 = bf16[160,768]{1,0:T(8,128)(2,1)S(1)} collective-permute-done((bf16[160,768]{1,0:T(8,128)(2,1)S(1)}, bf16[160,768]{1,0:T(8,128)(2,1)S(1)}, u32[]{:S(2)}, u32[]{:S(2)}) %collective-permute-start.24) | collective-permute-done | bytes 245792 | tf_op jit(solution)/shard_map/ppermute | solution.py:105
  175.7 3.4 %collective-permute-start.34 = (bf16[160,768]{1,0:T(8,128)(2,1)S(1)}, bf16[160,768]{1,0:T(8,128)(2,1)S(1)}, u32[]{:S(2)}, u32[]{:S(2)}) collective-permute-start(bf16[160,768]{1,0:T(8,128)(2,1)S(1)} %get-tuple-element.20), channel_id=1, source_target_pairs={{0,2},{1,3},{2,4},{3,5},{8,10},{9,11},{10,12},{11,13},{16,18},{17,... | collective-permute-start | bytes 737288 | tf_op jit(solution)/shard_map/ppermute | solution.py:90
  179.9 1.8 collective-permute-done.31
  182.1 1.0 collective-permute-done.34
  183.3 6.3 %collective-permute-start.35 = (bf16[160,768]{1,0:T(8,128)(2,1)S(1)}, bf16[160,768]{1,0:T(8,128)(2,1)S(1)}, u32[]{:S(2)}, u32[]{:S(2)}) collective-permute-start(bf16[160,768]{1,0:T(8,128)(2,1)S(1)} %get-tuple-element.28), channel_id=1, source_target_pairs={{0,2},{1,3},{2,4},{3,5},{4,6},{5,7},{8,10},{9,11},{10,12},{11,13},... | collective-permute-start | bytes 737288 | tf_op jit(solution)/shard_map/ppermute | solution.py:90
  189.7 1.3 collective-permute-start.37
  191.3 1.1 collective-permute-done.1
  193.4 4.4 %collective-permute-done.37 = bf16[160,768]{1,0:T(8,128)(2,1)S(1)} collective-permute-done((bf16[160,768]{1,0:T(8,128)(2,1)S(1)}, bf16[160,768]{1,0:T(8,128)(2,1)S(1)}, u32[]{:S(2)}, u32[]{:S(2)}) %collective-permute-start.37) | collective-permute-done | bytes 245792 | tf_op jit(solution)/shard_map/ppermute | solution.py:90
  (137 shorter events, 23.6 us)
Async XLA Ops:
  1.8 6.9 %collective-permute-start.4 = (f32[2,192]{1,0:T(2,128)S(1)}, f32[2,192]{1,0:T(2,128)S(1)}, u32[]{:S(2)}, u32[]{:S(2)}) collective-permute-start(f32[2,192]{1,0:T(2,128)S(1)} %pad_maximum_fusion.3), channel_id=1, source_target_pairs={{0,1},{1,0},{2,3},{3,2},{4,5},{5,4},{6,7},{7,6},{8,9},{9,8},{10,11... | collective-permute-start | bytes 4616 | tf_op jit(solution)/shard_map/ppermute | solution.py:151
  8.7 8.4 %collective-permute-start.5 = (f32[2,192]{1,0:T(2,128)S(1)}, f32[2,192]{1,0:T(2,128)S(1)}, u32[]{:S(2)}, u32[]{:S(2)}) collective-permute-start(f32[2,192]{1,0:T(2,128)S(1)} %fusion.129), channel_id=1, source_target_pairs={{0,2},{1,3},{2,0},{3,1},{4,6},{5,7},{6,4},{7,5},{8,10},{9,11},{10,... | collective-permute-start | bytes 4616 | tf_op jit(solution)/shard_map/ppermute | solution.py:154
  17.2 19.5 %collective-permute-start.13 = (bf16[384,3072]{1,0:T(8,128)(2,1)}, bf16[384,3072]{1,0:T(8,128)(2,1)}, u32[]{:S(2)}, u32[]{:S(2)}) collective-permute-start(bf16[384,3072]{1,0:T(8,128)(2,1)} %get-tuple-element.23), channel_id=1, source_target_pairs={{0,8},{8,0},{1,9},{9,1},{2,10},{10,2},{3,11},{11,3},{4,12},{12,4},... | collective-permute-start | bytes 7077896 | tf_op jit(solution)/shard_map/ppermute | solution.py:15
  17.2 6.6 %collective-permute-start.6 = (f32[2,192]{1,0:T(2,128)S(1)}, f32[2,192]{1,0:T(2,128)S(1)}, u32[]{:S(2)}, u32[]{:S(2)}) collective-permute-start(f32[2,192]{1,0:T(2,128)S(1)} %fusion.143), channel_id=1, source_target_pairs={{0,4},{1,5},{2,6},{3,7},{4,0},{5,1},{6,2},{7,3},{8,12},{9,13},{10,... | collective-permute-start | bytes 4616 | tf_op jit(solution)/shard_map/ppermute | solution.py:154
  19.9 3.9 %collective-permute-start.2 = (bf16[208,384]{1,0:T(8,128)(2,1)S(1)}, bf16[208,384]{1,0:T(8,128)(2,1)S(1)}, u32[]{:S(2)}, u32[]{:S(2)}) collective-permute-start(bf16[208,384]{1,0:T(8,128)(2,1)S(1)} %get-tuple-element.30), channel_id=1, source_target_pairs={{0,0},{1,2},{2,4},{3,6},{4,1},{5,3},{6,5},{7,7},{8,8},{9,10},{10,1... | collective-permute-start | bytes 479240 | tf_op jit(solution)/shard_map/ppermute | solution.py:146
  20.6 11.8 %collective-permute-start.3 = (bf16[208,384]{1,0:T(8,128)(2,1)S(1)}, bf16[208,384]{1,0:T(8,128)(2,1)S(1)}, u32[]{:S(2)}, u32[]{:S(2)}) collective-permute-start(bf16[208,384]{1,0:T(8,128)(2,1)S(1)} %get-tuple-element.31), channel_id=1, source_target_pairs={{0,1},{1,3},{2,5},{3,7},{4,0},{5,2},{6,4},{7,6},{8,9},{9,11},{10,1... | collective-permute-start | bytes 479240 | tf_op jit(solution)/shard_map/ppermute | solution.py:147
  23.8 20.5 %collective-permute-start.9 = (bf16[384,3072]{1,0:T(8,128)(2,1)}, bf16[384,3072]{1,0:T(8,128)(2,1)}, u32[]{:S(2)}, u32[]{:S(2)}) collective-permute-start(bf16[384,3072]{1,0:T(8,128)(2,1)} %get-tuple-element.25), channel_id=1, source_target_pairs={{0,8},{8,0},{1,9},{9,1},{2,10},{10,2},{3,11},{11,3},{4,12},{12,4},... | collective-permute-start | bytes 7077896 | tf_op jit(solution)/shard_map/ppermute | solution.py:15
  32.7 1.8 collective-permute-start.7
  33.9 39.2 %collective-permute-start.12 = (bf16[384,3072]{1,0:T(8,128)(2,1)}, bf16[384,3072]{1,0:T(8,128)(2,1)}, u32[]{:S(2)}, u32[]{:S(2)}) collective-permute-start(bf16[384,3072]{1,0:T(8,128)(2,1)} %get-tuple-element.24), channel_id=1, source_target_pairs={{0,8},{8,0},{1,9},{9,1},{2,10},{10,2},{3,11},{11,3},{4,12},{12,4},... | collective-permute-start | bytes 7077896 | tf_op jit(solution)/shard_map/ppermute | solution.py:15
  39.6 24.9 %collective-permute-start.14 = (bf16[320,1536]{1,0:T(8,128)(2,1)}, bf16[320,1536]{1,0:T(8,128)(2,1)}, u32[]{:S(2)}, u32[]{:S(2)}) collective-permute-start(bf16[320,1536]{1,0:T(8,128)(2,1)} %fusion.10), channel_id=1, source_target_pairs={{0,1},{1,0},{2,3},{3,2},{4,5},{5,4},{6,7},{7,6},{8,9},{9,8},{10,11... | collective-permute-start | bytes 2949128 | tf_op jit(solution)/shard_map/ppermute | solution.py:105
  40.4 57.8 %collective-permute-start.8 = (bf16[384,3072]{1,0:T(8,128)(2,1)S(1)}, bf16[384,3072]{1,0:T(8,128)(2,1)S(1)}, u32[]{:S(2)}, u32[]{:S(2)}) collective-permute-start(bf16[384,3072]{1,0:T(8,128)(2,1)S(1)} %get-tuple-element.22), channel_id=1, source_target_pairs={{0,8},{8,0},{1,9},{9,1},{2,10},{10,2},{3,11},{11,3},{4,12},{12,4},... | collective-permute-start | bytes 7077896 | tf_op jit(solution)/shard_map/ppermute | solution.py:15
  46.3 39.2 %collective-permute-start.10 = (bf16[320,1536]{1,0:T(8,128)(2,1)S(1)}, bf16[320,1536]{1,0:T(8,128)(2,1)S(1)}, u32[]{:S(2)}, u32[]{:S(2)}) collective-permute-start(bf16[320,1536]{1,0:T(8,128)(2,1)S(1)} %fusion.8), channel_id=1, source_target_pairs={{0,1},{1,0},{2,3},{3,2},{4,5},{5,4},{6,7},{7,6},{8,9},{9,8},{10,11... | collective-permute-start | bytes 2949128 | tf_op jit(solution)/shard_map/ppermute | solution.py:105
  66.8 21.8 %collective-permute-start.16 = (bf16[320,1536]{1,0:T(8,128)(2,1)S(1)}, bf16[320,1536]{1,0:T(8,128)(2,1)S(1)}, u32[]{:S(2)}, u32[]{:S(2)}) collective-permute-start(bf16[320,1536]{1,0:T(8,128)(2,1)S(1)} %get-tuple-element.42), channel_id=1, source_target_pairs={{0,2},{1,3},{6,4},{7,5},{8,10},{9,11},{14,12},{15,13},{16,18},{17,... | collective-permute-start | bytes 2949128 | tf_op jit(solution)/shard_map/ppermute | solution.py:90
  75.1 31.5 %collective-permute-start.15 = (bf16[320,1536]{1,0:T(8,128)(2,1)S(1)}, bf16[320,1536]{1,0:T(8,128)(2,1)S(1)}, u32[]{:S(2)}, u32[]{:S(2)}) collective-permute-start(bf16[320,1536]{1,0:T(8,128)(2,1)S(1)} %fusion.9), channel_id=1, source_target_pairs={{0,1},{1,0},{2,3},{3,2},{4,5},{5,4},{6,7},{7,6},{8,9},{9,8},{10,11... | collective-permute-start | bytes 2949128 | tf_op jit(solution)/shard_map/ppermute | solution.py:105
  89.1 22.9 %collective-permute-start.17 = (bf16[320,1536]{1,0:T(8,128)(2,1)S(1)}, bf16[320,1536]{1,0:T(8,128)(2,1)S(1)}, u32[]{:S(2)}, u32[]{:S(2)}) collective-permute-start(bf16[320,1536]{1,0:T(8,128)(2,1)S(1)} %select_convert_fusion), channel_id=1, source_target_pairs={{0,2},{1,3},{2,4},{3,5},{8,10},{9,11},{10,12},{11,13},{16,18},{17,... | collective-permute-start | bytes 2949128 | tf_op jit(solution)/shard_map/ppermute | solution.py:90
  93.5 18.4 %collective-permute-start.19 = (bf16[320,1536]{1,0:T(8,128)(2,1)S(1)}, bf16[320,1536]{1,0:T(8,128)(2,1)S(1)}, u32[]{:S(2)}, u32[]{:S(2)}) collective-permute-start(bf16[320,1536]{1,0:T(8,128)(2,1)S(1)} %select_convert_fusion), channel_id=1, source_target_pairs={{6,4},{7,5},{4,2},{5,3},{14,12},{15,13},{12,10},{13,11},{22,20},{2... | collective-permute-start | bytes 2949128 | tf_op jit(solution)/shard_map/ppermute | solution.py:90
  99.6 27.6 %collective-permute-start.11 = (bf16[320,1536]{1,0:T(8,128)(2,1)S(1)}, bf16[320,1536]{1,0:T(8,128)(2,1)}, u32[]{:S(2)}, u32[]{:S(2)}) collective-permute-start(bf16[320,1536]{1,0:T(8,128)(2,1)S(1)} %fusion.7), channel_id=1, source_target_pairs={{0,1},{1,0},{2,3},{3,2},{4,5},{5,4},{6,7},{7,6},{8,9},{9,8},{10,11... | collective-permute-start | bytes 2949128 | tf_op jit(solution)/shard_map/ppermute | solution.py:105
  108.6 16.4 %copy-start.3 = (bf16[1536]{0:T(1024)(128)(2,1)S(1)}, bf16[1536]{0:T(1024)(128)(2,1)}, u32[]{:S(2)}) copy-start(bf16[1536]{0:T(1024)(128)(2,1)} %param.12) | copy-start | bytes 9220
  113.6 24.3 %collective-permute-start.18 = (bf16[320,1536]{1,0:T(8,128)(2,1)}, bf16[320,1536]{1,0:T(8,128)(2,1)}, u32[]{:S(2)}, u32[]{:S(2)}) collective-permute-start(bf16[320,1536]{1,0:T(8,128)(2,1)} %get-tuple-element.26), channel_id=1, source_target_pairs={{0,2},{1,3},{2,4},{3,5},{4,6},{5,7},{8,10},{9,11},{10,12},{11,13},... | collective-permute-start | bytes 2949128 | tf_op jit(solution)/shard_map/ppermute | solution.py:90
  120.9 21.9 %collective-permute-start.20 = (bf16[320,1536]{1,0:T(8,128)(2,1)S(1)}, bf16[320,1536]{1,0:T(8,128)(2,1)}, u32[]{:S(2)}, u32[]{:S(2)}) collective-permute-start(bf16[320,1536]{1,0:T(8,128)(2,1)S(1)} %get-tuple-element.27), channel_id=1, source_target_pairs={{6,4},{7,5},{4,2},{5,3},{2,0},{3,1},{14,12},{15,13},{12,10},{13,11... | collective-permute-start | bytes 2949128 | tf_op jit(solution)/shard_map/ppermute | solution.py:90
  122.3 68.8 %collective-permute-start = (s32[192]{0:T(256)S(1)}, s32[192]{0:T(256)S(1)}, u32[]{:S(2)}, u32[]{:S(2)}) collective-permute-start(s32[192]{0:T(256)S(1)} %copy-done.6), channel_id=1, source_target_pairs={{0,8},{8,0},{1,9},{9,1},{2,10},{10,2},{3,11},{11,3},{4,12},{12,4},... | collective-permute-start | bytes 2312 | tf_op jit(solution)/shard_map/ppermute | solution.py:15
  125.0 17.8 %copy-start.2 = (bf16[384,3072]{1,0:T(8,128)(2,1)S(1)}, bf16[384,3072]{1,0:T(8,128)(2,1)}, u32[]{:S(2)}) copy-start(bf16[384,3072]{1,0:T(8,128)(2,1)} %copy-done.1) | copy-start | bytes 7077892
  125.0 24.5 %slice-start.1 = ((s8[18874368]{0:T(1024)(128)(4,1)}), s8[4194304]{0:T(1024)(128)(4,1)S(1)}, s32[]{:S(2)}) async-start(s8[18874368]{0:T(1024)(128)(4,1)} %bitcast.31), calls=%async_computation.1 | async-start | bytes 8388608
  127.1 22.4 %slice-start.2 = ((s8[18874368]{0:T(1024)(128)(4,1)}), s8[4194304]{0:T(1024)(128)(4,1)S(1)}, s32[]{:S(2)}) async-start(s8[18874368]{0:T(1024)(128)(4,1)} %bitcast.31), calls=%async_computation.2 | async-start | bytes 8388608
  127.1 22.4 %slice-start.3 = ((s8[18874368]{0:T(1024)(128)(4,1)}), s8[4194304]{0:T(1024)(128)(4,1)S(1)}, s32[]{:S(2)}) async-start(s8[18874368]{0:T(1024)(128)(4,1)} %bitcast.31), calls=%async_computation.3 | async-start | bytes 8388608
  127.1 22.4 %slice-start.4 = ((s8[18874368]{0:T(1024)(128)(4,1)}), s8[4194304]{0:T(1024)(128)(4,1)S(1)}, s32[]{:S(2)}) async-start(s8[18874368]{0:T(1024)(128)(4,1)} %bitcast.31), calls=%async_computation.4 | async-start | bytes 8388608
  127.2 22.4 %slice-start.5 = ((s8[18874368]{0:T(1024)(128)(4,1)}), s8[2097152]{0:T(1024)(128)(4,1)S(1)}, s32[]{:S(2)}) async-start(s8[18874368]{0:T(1024)(128)(4,1)} %bitcast.31), calls=%async_computation.5 | async-start | bytes 4194304
  150.5 28.5 %collective-permute-start.22 = (f32[160,768]{1,0:T(8,128)S(1)}, f32[160,768]{1,0:T(8,128)S(1)}, u32[]{:S(2)}, u32[]{:S(2)}) collective-permute-start(f32[160,768]{1,0:T(8,128)S(1)} %slice.222), channel_id=1, source_target_pairs={{0,8},{8,0},{1,9},{9,1},{2,10},{10,2},{3,11},{11,3},{4,12},{12,4},... | collective-permute-start | bytes 1474568 | tf_op jit(solution)/shard_map/ppermute | solution.py:15
  151.6 7.4 %collective-permute-start.23 = (f32[160,768]{1,0:T(8,128)S(1)}, f32[160,768]{1,0:T(8,128)S(1)}, u32[]{:S(2)}, u32[]{:S(2)}) collective-permute-start(f32[160,768]{1,0:T(8,128)S(1)} %slice.224), channel_id=1, source_target_pairs={{0,8},{8,0},{1,9},{9,1},{2,10},{10,2},{3,11},{11,3},{4,12},{12,4},... | collective-permute-start | bytes 1474568 | tf_op jit(solution)/shard_map/ppermute | solution.py:15
  153.1 14.8 %collective-permute-start.28 = (f32[160,768]{1,0:T(8,128)S(1)}, f32[160,768]{1,0:T(8,128)S(1)}, u32[]{:S(2)}, u32[]{:S(2)}) collective-permute-start(f32[160,768]{1,0:T(8,128)S(1)} %slice.230), channel_id=1, source_target_pairs={{0,8},{8,0},{1,9},{9,1},{2,10},{10,2},{3,11},{11,3},{4,12},{12,4},... | collective-permute-start | bytes 1474568 | tf_op jit(solution)/shard_map/ppermute | solution.py:15
  154.2 4.7 %collective-permute-start.29 = (f32[160,768]{1,0:T(8,128)S(1)}, f32[160,768]{1,0:T(8,128)S(1)}, u32[]{:S(2)}, u32[]{:S(2)}) collective-permute-start(f32[160,768]{1,0:T(8,128)S(1)} %slice.232), channel_id=1, source_target_pairs={{0,8},{8,0},{1,9},{9,1},{2,10},{10,2},{3,11},{11,3},{4,12},{12,4},... | collective-permute-start | bytes 1474568 | tf_op jit(solution)/shard_map/ppermute | solution.py:15
  158.9 1.9 collective-permute-start.32
  159.0 8.4 %collective-permute-start.30 = (bf16[160,768]{1,0:T(8,128)(2,1)S(1)}, bf16[160,768]{1,0:T(8,128)(2,1)S(1)}, u32[]{:S(2)}, u32[]{:S(2)}) collective-permute-start(bf16[160,768]{1,0:T(8,128)(2,1)S(1)} %fusion.66), channel_id=1, source_target_pairs={{0,1},{1,0},{2,3},{3,2},{4,5},{5,4},{6,7},{7,6},{8,9},{9,8},{10,11... | collective-permute-start | bytes 737288 | tf_op jit(solution)/shard_map/ppermute | solution.py:105
  160.8 8.6 %collective-permute-start.26 = (f32[160,768]{1,0:T(8,128)S(1)}, f32[160,768]{1,0:T(8,128)S(1)}, u32[]{:S(2)}, u32[]{:S(2)}) collective-permute-start(f32[160,768]{1,0:T(8,128)S(1)} %slice.226), channel_id=1, source_target_pairs={{0,8},{8,0},{1,9},{9,1},{2,10},{10,2},{3,11},{11,3},{4,12},{12,4},... | collective-permute-start | bytes 1474568 | tf_op jit(solution)/shard_map/ppermute | solution.py:15
  167.4 7.6 %collective-permute-start.24 = (bf16[160,768]{1,0:T(8,128)(2,1)S(1)}, bf16[160,768]{1,0:T(8,128)(2,1)S(1)}, u32[]{:S(2)}, u32[]{:S(2)}) collective-permute-start(bf16[160,768]{1,0:T(8,128)(2,1)S(1)} %fusion.70), channel_id=1, source_target_pairs={{0,1},{1,0},{2,3},{3,2},{4,5},{5,4},{6,7},{7,6},{8,9},{9,8},{10,11... | collective-permute-start | bytes 737288 | tf_op jit(solution)/shard_map/ppermute | solution.py:105
  168.0 7.5 %collective-permute-start.33 = (bf16[160,768]{1,0:T(8,128)(2,1)S(1)}, bf16[160,768]{1,0:T(8,128)(2,1)S(1)}, u32[]{:S(2)}, u32[]{:S(2)}) collective-permute-start(bf16[160,768]{1,0:T(8,128)(2,1)S(1)} %fusion.102), channel_id=1, source_target_pairs={{0,2},{1,3},{6,4},{7,5},{8,10},{9,11},{14,12},{15,13},{16,18},{17,... | collective-permute-start | bytes 737288 | tf_op jit(solution)/shard_map/ppermute | solution.py:90
  169.4 10.4 %collective-permute-start.27 = (f32[160,768]{1,0:T(8,128)S(1)}, f32[160,768]{1,0:T(8,128)S(1)}, u32[]{:S(2)}, u32[]{:S(2)}) collective-permute-start(f32[160,768]{1,0:T(8,128)S(1)} %slice.228), channel_id=1, source_target_pairs={{0,8},{8,0},{1,9},{9,1},{2,10},{10,2},{3,11},{11,3},{4,12},{12,4},... | collective-permute-start | bytes 1474568 | tf_op jit(solution)/shard_map/ppermute | solution.py:15
  175.0 6.7 %collective-permute-start.31 = (bf16[160,768]{1,0:T(8,128)(2,1)S(1)}, bf16[160,768]{1,0:T(8,128)(2,1)S(1)}, u32[]{:S(2)}, u32[]{:S(2)}) collective-permute-start(bf16[160,768]{1,0:T(8,128)(2,1)S(1)} %fusion.67), channel_id=1, source_target_pairs={{0,1},{1,0},{2,3},{3,2},{4,5},{5,4},{6,7},{7,6},{8,9},{9,8},{10,11... | collective-permute-start | bytes 737288 | tf_op jit(solution)/shard_map/ppermute | solution.py:105
  175.6 22.1 %slice-start = ((bf16[192,768]{1,0:T(8,128)(2,1)}), bf16[128,768]{1,0:T(8,128)(2,1)S(1)}, s32[]{:S(2)}) async-start(bf16[192,768]{1,0:T(8,128)(2,1)} %param.8), calls=%async_computation | async-start | bytes 393216 | tf_op jit(solution)/shard_map/slice | solution.py:242
  175.7 7.5 %collective-permute-start.34 = (bf16[160,768]{1,0:T(8,128)(2,1)S(1)}, bf16[160,768]{1,0:T(8,128)(2,1)S(1)}, u32[]{:S(2)}, u32[]{:S(2)}) collective-permute-start(bf16[160,768]{1,0:T(8,128)(2,1)S(1)} %get-tuple-element.20), channel_id=1, source_target_pairs={{0,2},{1,3},{2,4},{3,5},{8,10},{9,11},{10,12},{11,13},{16,18},{17,... | collective-permute-start | bytes 737288 | tf_op jit(solution)/shard_map/ppermute | solution.py:90
  179.1 4.1 %collective-permute-start.36 = (bf16[160,768]{1,0:T(8,128)(2,1)S(1)}, bf16[160,768]{1,0:T(8,128)(2,1)S(1)}, u32[]{:S(2)}, u32[]{:S(2)}) collective-permute-start(bf16[160,768]{1,0:T(8,128)(2,1)S(1)} %get-tuple-element.20), channel_id=1, source_target_pairs={{6,4},{7,5},{4,2},{5,3},{14,12},{15,13},{12,10},{13,11},{22,20},{2... | collective-permute-start | bytes 737288 | tf_op jit(solution)/shard_map/ppermute | solution.py:90
  179.8 12.6 %collective-permute-start.21 = (f32[160,768]{1,0:T(8,128)S(1)}, f32[160,768]{1,0:T(8,128)S(1)}, u32[]{:S(2)}, u32[]{:S(2)}) collective-permute-start(f32[160,768]{1,0:T(8,128)S(1)} %slice.220), channel_id=1, source_target_pairs={{0,8},{8,0},{1,9},{9,1},{2,10},{10,2},{3,11},{11,3},{4,12},{12,4},... | collective-permute-start | bytes 1474568 | tf_op jit(solution)/shard_map/ppermute | solution.py:15
  181.7 10.7 %collective-permute-start.25 = (bf16[160,768]{1,0:T(8,128)(2,1)S(1)}, bf16[160,768]{1,0:T(8,128)(2,1)S(1)}, u32[]{:S(2)}, u32[]{:S(2)}) collective-permute-start(bf16[160,768]{1,0:T(8,128)(2,1)S(1)} %fusion.71), channel_id=1, source_target_pairs={{0,1},{1,0},{2,3},{3,2},{4,5},{5,4},{6,7},{7,6},{8,9},{9,8},{10,11... | collective-permute-start | bytes 737288 | tf_op jit(solution)/shard_map/ppermute | solution.py:105
  183.3 10.0 %collective-permute-start.35 = (bf16[160,768]{1,0:T(8,128)(2,1)S(1)}, bf16[160,768]{1,0:T(8,128)(2,1)S(1)}, u32[]{:S(2)}, u32[]{:S(2)}) collective-permute-start(bf16[160,768]{1,0:T(8,128)(2,1)S(1)} %get-tuple-element.28), channel_id=1, source_target_pairs={{0,2},{1,3},{2,4},{3,5},{4,6},{5,7},{8,10},{9,11},{10,12},{11,13},... | collective-permute-start | bytes 737288 | tf_op jit(solution)/shard_map/ppermute | solution.py:90
  189.7 8.1 %collective-permute-start.37 = (bf16[160,768]{1,0:T(8,128)(2,1)S(1)}, bf16[160,768]{1,0:T(8,128)(2,1)S(1)}, u32[]{:S(2)}, u32[]{:S(2)}) collective-permute-start(bf16[160,768]{1,0:T(8,128)(2,1)S(1)} %get-tuple-element.29), channel_id=1, source_target_pairs={{6,4},{7,5},{4,2},{5,3},{2,0},{3,1},{14,12},{15,13},{12,10},{13,11... | collective-permute-start | bytes 737288 | tf_op jit(solution)/shard_map/ppermute | solution.py:90
  191.1 1.3 collective-permute-start.1
  198.2 1.2 collective-permute-start.39
  198.3 1.8 collective-permute-start.38
  (5 other events, 54.8 us)

commit v3 on v2

--- a/solution.py
+++ b/solution.py
@@ -1,6 +1,8 @@
 import jax
 import jax.numpy as jnp
 from jax import lax
+from jax.experimental import pallas as pl
+from jax.experimental.pallas import tpu as pltpu
 from jax.sharding import PartitionSpec as P
 
 SEND = 32
@@ -71,6 +73,7 @@
 
 
 ACROSS = [(i, i ^ 1) for i in range(8)]
+DIRECT_ORDER = tuple(tuple(z ^ (3 - i) for i in range(4)) for z in range(4))
 ORDER = ((3, 2, 1, 0), (3, 2, 0, 1), (0, 1, 3, 2), (0, 1, 2, 3))
 DEPTH = 2
 
@@ -92,6 +95,49 @@
 
 def after(array, other):
     return lax.optimization_barrier((array, other))[0]
+
+
+COST = pl.CostEstimate(flops=0, bytes_accessed=0, transcendentals=0)
+
+
+def pieces(weight, starts, width, count):
+    depth, each = weight.shape[0], starts.shape[0] // count
+
+    def kernel(starts_ref, weight_ref, *rest):
+        outs, (held, come, leave) = rest[:count], rest[count:]
+        comes, leaves = [], []
+        for i in range(count * each):
+            begin = pl.multiple_of(starts_ref[i], 128)
+            place = held.at[i // each, :, pl.ds(i % each * width, width)]
+            comes.append(
+                pltpu.make_async_copy(weight_ref.at[:, pl.ds(begin, width)], place, come.at[i])
+            )
+            comes[-1].start()
+        for i in range(count):
+            for copy in comes[i * each : (i + 1) * each]:
+                copy.wait()
+            leaves.append(pltpu.make_async_copy(held.at[i], outs[i], leave.at[i]))
+            leaves[-1].start()
+        for copy in leaves:
+            copy.wait()
+
+    shape = (depth, each * width)
+    return pl.pallas_call(
+        kernel,
+        out_shape=[jax.ShapeDtypeStruct(shape, weight.dtype)] * count,
+        in_specs=[
+            pl.BlockSpec(memory_space=pltpu.SMEM),
+            pl.BlockSpec(memory_space=pltpu.HBM),
+        ],
+        out_specs=[pl.BlockSpec(memory_space=pltpu.HBM)] * count,
+        scratch_shapes=[
+            pltpu.VMEM((count, *shape), weight.dtype),
+            pltpu.SemaphoreType.DMA((count * each,)),
+            pltpu.SemaphoreType.DMA((count,)),
+        ],
+        compiler_params=pltpu.CompilerParams(vmem_limit_bytes=40 << 20),
+        cost_estimate=COST,
+    )(starts, weight)
 
 
 class Across:
@@ -107,14 +153,19 @@
 
 
 class Scatter:
-    def __init__(self, across, block, z):
+    def __init__(self, across, block, z, direct=False):
         self.across, self.block, self.z = across, block, z
-        self.kept = []
+        self.kept, self.direct = [], direct
 
     def step(self):
         step, z, kept = len(self.kept), self.z, self.kept
         sent, own = self.block(step)
         kept.append(own + self.across.send(sent))
+        if self.direct:
+            if step < 3:
+                kept[-1] = shift(kept[-1], along_z(*((i, i ^ (3 - step)) for i in range(4))))
+                return None
+            return (kept[0] + kept[1]) + (kept[2] + kept[3])
         if step == 0:
             self.first = shift(kept[0], ENDS_IN)
         elif step == 1:
@@ -137,6 +188,7 @@
     dp, mp = lax.axis_index("dp"), lax.axis_index("mp")
     x, z = lax.rem(mp, 2), mp // 2
     order = jnp.asarray(ORDER, jnp.int32)[z]
+    outer_order = jnp.asarray(DIRECT_ORDER, jnp.int32)[z]
     loaded = row_image[KEEP] < IMAGES
 
     sheet = jnp.concatenate([tokens, jnp.broadcast_to(norm_gain[None, :], (16, cols))], axis=0)
@@ -149,9 +201,11 @@
     values = tokens.astype(jnp.float32)
     moments = jnp.stack([jnp.sum(values, axis=1), jnp.sum(values * values, axis=1)])
     moments = moments + lax.ppermute(moments, "mp", [(i, i ^ 1) for i in range(8)])
-    inner_weight = after(inner_weight, moments)
-    for bit in (2, 4):
-        moments = moments + lax.ppermute(moments, "mp", [(i, i ^ bit) for i in range(8)])
+    moments, same, other = lax.optimization_barrier((moments, same, other))
+    gate = moments
+    moments = moments + sum(
+        lax.ppermute(moments, "mp", [(i, i ^ bit) for i in range(8)]) for bit in (2, 4, 6)
+    )
     row_mean = (moments[0] / width)[:, None]
     row_var = (moments[1] / width)[:, None] - row_mean * row_mean
     scale = lax.rsqrt(row_var + EPSILON)
@@ -182,9 +236,16 @@
     pair = units // 8
     one = pair // 2
     lent = []
-    for step in range(4):
-        start = (1 - dp) * (units // 2) + order[step] * pair
-        lent.append(swap_dp(lax.dynamic_slice_in_dim(inner_weight, start, pair, 1)))
+
+    def lend(step, gate):
+        start = after((1 - dp) * (units // 2) + order[step] * pair, gate)
+        if step < 2:
+            strip = pieces(inner_weight, start.reshape(1), pair, 1)[0]
+        else:
+            strip = lax.dynamic_slice_in_dim(inner_weight, start, pair, 1)
+        lent.append(swap_dp(strip))
+
+    lend(0, gate)
 
     def inner_block(rows):
         def block(step):
@@ -197,19 +258,29 @@
                     rows[:, :features], mine, preferred_element_type=jnp.float32
                 ) + jnp.dot(rows[:, features:], got, preferred_element_type=jnp.float32)
 
-            return product(1 - x), product(x)
+            sent = product(1 - x)
+            if step < 3:
+                lend(step + 1, gate)
+            return sent, product(x)
 
         return block
 
     def outer_block(hidden):
         mine = hidden.shape[0] // 2
+        gates = []
 
         def block(step):
+            given = hidden
+            if step >= 2:
+                given = after(hidden, gates[0])
+
             def product(side):
-                start = order[step] * 2 * cols + side * cols
+                start = outer_order[step] * 2 * cols + side * cols
                 weight = lax.dynamic_slice_in_dim(outer_weight, start, cols, 1)
-                out = jnp.dot(hidden, weight, preferred_element_type=jnp.float32)
-                return out[:mine] + swap_dp(out[mine:])
+                out = jnp.dot(given, weight, preferred_element_type=jnp.float32)
+                got = swap_dp(out[mine:])
+                gates.append(got)
+                return out[:mine] + got
 
             return product(1 - x), product(x)
 
@@ -231,7 +302,7 @@
                     branch_out.append(outer[-1].step())
             elif i and step == 1:
                 outer[-1].step()
-        outer.append(Scatter(across, outer_block(activate(pre_act)), z))
+        outer.append(Scatter(across, outer_block(activate(pre_act)), z, direct=True))
     for step in range(4):
         branch_out.append(outer[-1].step())
     branch_out = jnp.concatenate([part for part in branch_out if part is not None], axis=0)

time: 202 us -> 199 us (0.985)
  starting transfers between devices: 48.7 us -> 40.8 us
  Pallas kernels: 0 us -> 4.96 us
  waiting for transfers between devices: 84.9 us -> 81.1 us
  local copies, waits for them, and re-layouts: 9.82 us -> 12.6 us
    ppermute x10 -> x8, starting transfers between devices: 29.4 us -> 15.3 us  [shift(): lax.ppermute(array.astype(jnp.bfloat16), 'mp', moves).astype(jnp.float32)]
    ppermute x1, waiting for transfers between devices: 8.54 us -> 0.01 us  [eight(): lax.ppermute(other, 'mp', [(4 * e + q, 2 * q + 1 - e) for e in (0, 1) for...]
    pallas_call x0 -> x2, Pallas kernels: none -> 4.96 us  [pieces(): pl.pallas_call(kernel, out_shape=[jax.ShapeDtypeStruct(shape, weight.dtyp...]
    ppermute x10 -> x8, waiting for transfers between devices: 26.5 us -> 31.1 us  [shift(): lax.ppermute(array.astype(jnp.bfloat16), 'mp', moves).astype(jnp.float32)]
    ppermute x1, starting transfers between devices: 3.2 us -> 5.77 us  [eight(): lax.ppermute(other, 'mp', [(4 * e + q, 2 * q + 1 - e) for e in (0, 1) for...]
    ppermute x8, starting transfers between devices: 5.13 us -> 7.19 us  [send(): self.done.append(lax.ppermute(array, 'mp', ACROSS))]
    dynamic_slice x1 -> x2, local copies, waits for them, and re-layouts: 6.79 us -> 7.46 us  [the longest x1 6.78 us: lend(): strip = lax.dynamic_slice_in_dim(inner_weight, start, pair, 1)]
    ppermute x2 -> x3, starting transfers between devices: 4.3 us -> 4.45 us  [eight(): lax.ppermute(moments, 'mp', [(i, i ^ bit) for i in range(8)])]
  transfers between devices with their start and end apart: 40 -> 39, of which waited for: 17 -> 15; matrix products, arithmetic and copies ran while one was open for 28% -> 30% of each run, Pallas kernels for 0% -> 3%
where the time goes in v3:
time: 199 us; the launch traced here: 198 us
  waiting for transfers between devices  81.1 us (41%)
  matrix products  43.9 us (22%)
  starting transfers between devices  40.8 us (21%)
  local copies, waits for them, and re-layouts  12.6 us (6%)
  between operations  7.33 us (4%)
  other arithmetic  7.27 us (4%)
  Pallas kernels  4.96 us (2%)
    ppermute x8, waiting for transfers between devices, send(): self.done.append(lax.ppermute(array, 'mp', ACROSS))  48.2 us
    ppermute x8, waiting for transfers between devices, shift(): lax.ppermute(array.astype(jnp.bfloat16), 'mp', moves).astype(jnp.float32)  31.1 us
    dot_general x8, matrix products, product(): jnp.dot(rows[:, features:], got, preferred_element_type=jnp.float32)  20.5 us
    dot_general x8, matrix products, product(): jnp.dot(rows[:, :features], mine, preferred_element_type=jnp.float32)  15.7 us
    ppermute x8, starting transfers between devices, shift(): lax.ppermute(array.astype(jnp.bfloat16), 'mp', moves).astype(jnp.float32)  15.3 us
    dot_general x8, matrix products, product(): out = jnp.dot(given, weight, preferred_element_type=jnp.float32)  7.67 us
    ppermute x8, starting transfers between devices, send(): self.done.append(lax.ppermute(array, 'mp', ACROSS))  7.19 us
    dynamic_slice x1, local copies, waits for them, and re-layouts, lend(): strip = lax.dynamic_slice_in_dim(inner_weight, start, pair, 1)  6.78 us
  transfers between devices with their start and end apart: 39, of which 15 were waited for; matrix products, arithmetic and copies ran while one was open for 30% of the time, Pallas kernels for 3%

profile of v3, /device:TPU:0, one launch (start us, length us, event | category | flops | bytes accessed | tf_op | source)
XLA Modules:
  0.0 198.0 jit_solution(2974061031370995115)
XLA Ops:
  1.3 1.0 fusion.87
  3.0 5.8 %collective-permute-start.4 = (bf16[208,384]{1,0:T(8,128)(2,1)S(1)}, bf16[208,384]{1,0:T(8,128)(2,1)S(1)}, u32[]{:S(2)}, u32[]{:S(2)}) collective-permute-start(bf16[208,384]{1,0:T(8,128)(2,1)S(1)} %get-tuple-element.38), channel_id=1, source_target_pairs={{0,1},{1,3},{2,5},{3,7},{4,0},{5,2},{6,4},{7,6},{8,9},{9,11},{10,1... | collective-permute-start | bytes 479240 | tf_op jit(solution)/shard_map/ppermute | solution.py:199
  8.8 1.2 convert_reduce_fusion
  10.0 2.7 %collective-permute-start.2 = (f32[2,192]{1,0:T(2,128)S(1)}, f32[2,192]{1,0:T(2,128)S(1)}, u32[]{:S(2)}, u32[]{:S(2)}) collective-permute-start(f32[2,192]{1,0:T(2,128)S(1)} %pad_maximum_fusion.3), channel_id=1, source_target_pairs={{0,1},{1,0},{2,3},{3,2},{4,5},{5,4},{6,7},{7,6},{8,9},{9,8},{10,11... | collective-permute-start | bytes 4616 | tf_op jit(solution)/shard_map/ppermute | solution.py:203
  15.3 1.3 slice.175
  18.6 1.9 collective-permute-start.6
  20.5 2.4 %collective-permute-start.7 = (f32[2,192]{1,0:T(2,128)S(1)}, f32[2,192]{1,0:T(2,128)S(1)}, u32[]{:S(2)}, u32[]{:S(2)}) collective-permute-start(f32[2,192]{1,0:T(2,128)S(1)} %fusion.131), channel_id=1, source_target_pairs={{0,6},{1,7},{2,4},{3,5},{4,2},{5,3},{6,0},{7,1},{8,14},{9,15},{10,... | collective-permute-start | bytes 4616 | tf_op jit(solution)/shard_map/ppermute | solution.py:207
  23.1 3.1 %shard_map.105 = bf16[384,3072]{1,0:T(8,128)(2,1)} custom-call(s32[1]{0:T(128)} %bitcast.10.starts_ref, bf16[384,24576]{1,0:T(8,128)(2,1)} %weight_ref.3), custom_call_target="tpu_custom_call" | custom-call | tf_op jit(solution)/shard_map/pallas_call | solution.py:125
  26.3 1.8 shard_map.104
  29.0 6.8 %constant_dynamic-slice_fusion.2 = (bf16[384,3072]{1,0:T(8,128)(2,1)}, bf16[384,3072]{1,0:T(8,128)(2,1)}) fusion(bf16[384,24576]{1,0:T(8,128)(2,1)} %weight_ref.3, s32[]{:T(128)S(6)} %select_n.163, s32[]{:T(128)S(6)} %select_n.171), kind=kLoop, calls=%fused_computation.181 | loop fusion | bytes 9437192 | tf_op jit(solution)/shard_map/dynamic_slice | solution.py:245
  36.5 1.9 fusion.41
  38.5 2.9 %fusion.10 = bf16[320,1536]{1,0:T(8,128)(2,1)} fusion(f32[320,1536]{1,0:T(8,128)S(1)} %fusion.41, bf16[384,3072]{1,0:T(8,128)(2,1)} %collective-permute-done.14, s32[]{:T(128)S(6)} %select_n.166, bf16[320,768]{1,0:T(8,128)(2,1)S(1)} %pad_maximum_fusion), kind=kOutput, calls=%fused_computation.19 | convolution fusion | flops 378470400 | bytes 4374532 | tf_op jit(solution)/shard_map/dot_general | solution.py:259
  41.5 1.9 fusion.38
  43.4 1.9 fusion.53
  45.4 2.0 fusion.8
  47.3 2.1 %collective-permute-start.11 = (bf16[320,1536]{1,0:T(8,128)(2,1)S(1)}, bf16[320,1536]{1,0:T(8,128)(2,1)S(1)}, u32[]{:S(2)}, u32[]{:S(2)}) collective-permute-start(bf16[320,1536]{1,0:T(8,128)(2,1)S(1)} %fusion.8), channel_id=1, source_target_pairs={{0,1},{1,0},{2,3},{3,2},{4,5},{5,4},{6,7},{7,6},{8,9},{9,8},{10,11... | collective-permute-start | bytes 2949128 | tf_op jit(solution)/shard_map/ppermute | solution.py:151
  49.4 17.0 %collective-permute-done.15 = bf16[320,1536]{1,0:T(8,128)(2,1)} collective-permute-done((bf16[320,1536]{1,0:T(8,128)(2,1)}, bf16[320,1536]{1,0:T(8,128)(2,1)}, u32[]{:S(2)}, u32[]{:S(2)}) %collective-permute-start.15) | collective-permute-done | bytes 983072 | tf_op jit(solution)/shard_map/ppermute | solution.py:151
  66.4 2.2 %fusion.135 = (bf16[320,1536]{1,0:T(8,128)(2,1)S(1)}, f32[320,1536]{1,0:T(8,128)S(1)}) fusion(bf16[320,1536]{1,0:T(8,128)(2,1)} %collective-permute-done.15, f32[320,1536]{1,0:T(8,128)S(1)} %fusion.38, bf16[384,3072]{1,0:T(8,128)(2,1)} %collective-permute-done.14, s32[]{:T(128)S(6)} %select_n.164, bf16[320,768]{1,0:T(8,128)(2,1)S(1)} %pad_maximum_fusion), kind=kOutput, calls=%fused_computation.196 | convolution fusion | flops 379453440 | bytes 7323652 | tf_op jit(solution)/shard_map/dot_general | solution.py:259
  68.6 1.4 collective-permute-start.17
  70.0 1.9 fusion.44
  71.9 1.9 fusion.50
  73.9 2.0 fusion.9
  76.5 10.8 %collective-permute-done.11 = bf16[320,1536]{1,0:T(8,128)(2,1)S(1)} collective-permute-done((bf16[320,1536]{1,0:T(8,128)(2,1)S(1)}, bf16[320,1536]{1,0:T(8,128)(2,1)S(1)}, u32[]{:S(2)}, u32[]{:S(2)}) %collective-permute-start.11) | collective-permute-done | bytes 983072 | tf_op jit(solution)/shard_map/ppermute | solution.py:151
  87.3 2.0 fusion.2
  90.2 4.4 %collective-permute-start.18 = (bf16[320,1536]{1,0:T(8,128)(2,1)S(1)}, bf16[320,1536]{1,0:T(8,128)(2,1)S(1)}, u32[]{:S(2)}, u32[]{:S(2)}) collective-permute-start(bf16[320,1536]{1,0:T(8,128)(2,1)S(1)} %select_convert_fusion), channel_id=1, source_target_pairs={{0,2},{1,3},{2,4},{3,5},{8,10},{9,11},{10,12},{11,13},{16,18},{17,... | collective-permute-start | bytes 2949128 | tf_op jit(solution)/shard_map/ppermute | solution.py:93
  95.5 1.9 fusion.47
  97.5 1.9 fusion.56
  101.4 7.0 %collective-permute-done.16 = bf16[320,1536]{1,0:T(8,128)(2,1)S(1)} collective-permute-done((bf16[320,1536]{1,0:T(8,128)(2,1)S(1)}, bf16[320,1536]{1,0:T(8,128)(2,1)S(1)}, u32[]{:S(2)}, u32[]{:S(2)}) %collective-permute-start.16) | collective-permute-done | bytes 983072 | tf_op jit(solution)/shard_map/ppermute | solution.py:151
  108.4 2.0 fusion.1
  110.4 2.9 %collective-permute-done.18 = bf16[320,1536]{1,0:T(8,128)(2,1)S(1)} collective-permute-done((bf16[320,1536]{1,0:T(8,128)(2,1)S(1)}, bf16[320,1536]{1,0:T(8,128)(2,1)S(1)}, u32[]{:S(2)}, u32[]{:S(2)}) %collective-permute-start.18) | collective-permute-done | bytes 983072 | tf_op jit(solution)/shard_map/ppermute | solution.py:93
  113.3 1.6 add_convert_fusion.1
  114.9 7.3 %collective-permute-start.19 = (bf16[320,1536]{1,0:T(8,128)(2,1)}, bf16[320,1536]{1,0:T(8,128)(2,1)}, u32[]{:S(2)}, u32[]{:S(2)}) collective-permute-start(bf16[320,1536]{1,0:T(8,128)(2,1)} %get-tuple-element.36), channel_id=1, source_target_pairs={{0,2},{1,3},{2,4},{3,5},{4,6},{5,7},{8,10},{9,11},{10,12},{11,13},... | collective-permute-start | bytes 2949128 | tf_op jit(solution)/shard_map/ppermute | solution.py:93
  122.2 1.3 collective-permute-start.21
  128.1 2.1 %fusion.59 = f32[320,1536]{1,0:T(8,128)S(1)} fusion(bf16[384,24576]{1,0:T(8,128)(2,1)} %weight_ref.3, s32[]{:T(128)S(6)} %select_n.162, bf16[320,768]{1,0:T(8,128)(2,1)S(1)} %pad_maximum_fusion), kind=kOutput, calls=%fused_computation.79 | convolution fusion | flops 377487360 | bytes 3391492 | tf_op jit(solution)/shard_map/dot_general | solution.py:257
  130.2 8.9 %collective-permute-done.19 = bf16[320,1536]{1,0:T(8,128)(2,1)} collective-permute-done((bf16[320,1536]{1,0:T(8,128)(2,1)}, bf16[320,1536]{1,0:T(8,128)(2,1)}, u32[]{:S(2)}, u32[]{:S(2)}) %collective-permute-start.19) | collective-permute-done | bytes 983072 | tf_op jit(solution)/shard_map/ppermute | solution.py:93
  139.1 4.8 %collective-permute-done.21 = bf16[320,1536]{1,0:T(8,128)(2,1)} collective-permute-done((bf16[320,1536]{1,0:T(8,128)(2,1)S(1)}, bf16[320,1536]{1,0:T(8,128)(2,1)}, u32[]{:S(2)}, u32[]{:S(2)}) %collective-permute-start.21) | collective-permute-done | bytes 983072 | tf_op jit(solution)/shard_map/ppermute | solution.py:93
  144.0 6.7 %fusion.29 = bf16[320,1536]{1,0:T(8,128)(2,1)S(1)} fusion(bf16[320,1536]{1,0:T(8,128)(2,1)} %collective-permute-done.21, bf16[320,1536]{1,0:T(8,128)(2,1)} %collective-permute-done.19, bf16[320,1536]{1,0:T(8,128)(2,1)} %collective-permute-done.12, f32[320,1536]{1,0:T(8,128)S(1)} %fusion.59, bf16[384,3072]{1,0:T(8,128)(2,1)S(1)} %copy-done.2, ...), kind=kOutput, calls=%fused_computation.38 | convolution fusion | flops 413368320 | bytes 7331844 | tf_op jit(solution)/shard_map/dot_general | solution.py:259
  151.8 1.0 fusion.25
  154.5 1.0 fusion.21
  158.2 1.0 fusion.17
  160.2 1.0 fusion.13
  161.3 1.2 collective-permute-start.28
  162.5 2.3 %collective-permute-done.24 = bf16[160,768]{1,0:T(8,128)(2,1)S(1)} collective-permute-done((bf16[160,768]{1,0:T(8,128)(2,1)S(1)}, bf16[160,768]{1,0:T(8,128)(2,1)S(1)}, u32[]{:S(2)}, u32[]{:S(2)}) %collective-permute-start.24) | collective-permute-done | bytes 245792 | tf_op jit(solution)/shard_map/ppermute | solution.py:151
  165.4 4.1 %collective-permute-done.28 = bf16[160,768]{1,0:T(8,128)(2,1)S(1)} collective-permute-done((bf16[160,768]{1,0:T(8,128)(2,1)S(1)}, bf16[160,768]{1,0:T(8,128)(2,1)S(1)}, u32[]{:S(2)}, u32[]{:S(2)}) %collective-permute-start.28) | collective-permute-done | bytes 245792 | tf_op jit(solution)/shard_map/ppermute | solution.py:151
  170.3 1.1 collective-permute-done.35
  172.4 7.0 %collective-permute-done.32 = bf16[160,768]{1,0:T(8,128)(2,1)S(1)} collective-permute-done((bf16[160,768]{1,0:T(8,128)(2,1)S(1)}, bf16[160,768]{1,0:T(8,128)(2,1)S(1)}, u32[]{:S(2)}, u32[]{:S(2)}) %collective-permute-start.32) | collective-permute-done | bytes 245792 | tf_op jit(solution)/shard_map/ppermute | solution.py:151
  180.7 2.1 %collective-permute-done.25 = bf16[160,768]{1,0:T(8,128)(2,1)S(1)} collective-permute-done((bf16[160,768]{1,0:T(8,128)(2,1)S(1)}, bf16[160,768]{1,0:T(8,128)(2,1)S(1)}, u32[]{:S(2)}, u32[]{:S(2)}) %collective-permute-start.25) | collective-permute-done | bytes 245792 | tf_op jit(solution)/shard_map/ppermute | solution.py:93
  182.8 12.0 %collective-permute-done.29 = bf16[160,768]{1,0:T(8,128)(2,1)S(1)} collective-permute-done((bf16[160,768]{1,0:T(8,128)(2,1)S(1)}, bf16[160,768]{1,0:T(8,128)(2,1)S(1)}, u32[]{:S(2)}, u32[]{:S(2)}) %collective-permute-start.29) | collective-permute-done | bytes 245792 | tf_op jit(solution)/shard_map/ppermute | solution.py:93
  (136 shorter events, 24.0 us)
Async XLA Ops:
  2.4 16.1 %collective-permute-start.3 = (bf16[208,384]{1,0:T(8,128)(2,1)S(1)}, bf16[208,384]{1,0:T(8,128)(2,1)S(1)}, u32[]{:S(2)}, u32[]{:S(2)}) collective-permute-start(bf16[208,384]{1,0:T(8,128)(2,1)S(1)} %get-tuple-element.39), channel_id=1, source_target_pairs={{0,0},{1,2},{2,4},{3,6},{4,1},{5,3},{6,5},{7,7},{8,8},{9,10},{10,1... | collective-permute-start | bytes 479240 | tf_op jit(solution)/shard_map/ppermute | solution.py:198
  3.0 15.4 %collective-permute-start.4 = (bf16[208,384]{1,0:T(8,128)(2,1)S(1)}, bf16[208,384]{1,0:T(8,128)(2,1)S(1)}, u32[]{:S(2)}, u32[]{:S(2)}) collective-permute-start(bf16[208,384]{1,0:T(8,128)(2,1)S(1)} %get-tuple-element.38), channel_id=1, source_target_pairs={{0,1},{1,3},{2,5},{3,7},{4,0},{5,2},{6,4},{7,6},{8,9},{9,11},{10,1... | collective-permute-start | bytes 479240 | tf_op jit(solution)/shard_map/ppermute | solution.py:199
  10.0 8.5 %collective-permute-start.2 = (f32[2,192]{1,0:T(2,128)S(1)}, f32[2,192]{1,0:T(2,128)S(1)}, u32[]{:S(2)}, u32[]{:S(2)}) collective-permute-start(f32[2,192]{1,0:T(2,128)S(1)} %pad_maximum_fusion.3), channel_id=1, source_target_pairs={{0,1},{1,0},{2,3},{3,2},{4,5},{5,4},{6,7},{7,6},{8,9},{9,8},{10,11... | collective-permute-start | bytes 4616 | tf_op jit(solution)/shard_map/ppermute | solution.py:203
  18.5 10.2 %collective-permute-start.5 = (f32[2,192]{1,0:T(2,128)S(1)}, f32[2,192]{1,0:T(2,128)S(1)}, u32[]{:S(2)}, u32[]{:S(2)}) collective-permute-start(f32[2,192]{1,0:T(2,128)S(1)} %fusion.131), channel_id=1, source_target_pairs={{0,2},{1,3},{2,0},{3,1},{4,6},{5,7},{6,4},{7,5},{8,10},{9,11},{10,... | collective-permute-start | bytes 4616 | tf_op jit(solution)/shard_map/ppermute | solution.py:207
  18.6 10.1 %collective-permute-start.6 = (f32[2,192]{1,0:T(2,128)S(1)}, f32[2,192]{1,0:T(2,128)S(1)}, u32[]{:S(2)}, u32[]{:S(2)}) collective-permute-start(f32[2,192]{1,0:T(2,128)S(1)} %fusion.131), channel_id=1, source_target_pairs={{0,4},{1,5},{2,6},{3,7},{4,0},{5,1},{6,2},{7,3},{8,12},{9,13},{10,... | collective-permute-start | bytes 4616 | tf_op jit(solution)/shard_map/ppermute | solution.py:207
  20.5 8.2 %collective-permute-start.7 = (f32[2,192]{1,0:T(2,128)S(1)}, f32[2,192]{1,0:T(2,128)S(1)}, u32[]{:S(2)}, u32[]{:S(2)}) collective-permute-start(f32[2,192]{1,0:T(2,128)S(1)} %fusion.131), channel_id=1, source_target_pairs={{0,6},{1,7},{2,4},{3,5},{4,2},{5,3},{6,0},{7,1},{8,14},{9,15},{10,... | collective-permute-start | bytes 4616 | tf_op jit(solution)/shard_map/ppermute | solution.py:207
  26.2 12.3 %collective-permute-start.14 = (bf16[384,3072]{1,0:T(8,128)(2,1)}, bf16[384,3072]{1,0:T(8,128)(2,1)}, u32[]{:S(2)}, u32[]{:S(2)}) collective-permute-start(bf16[384,3072]{1,0:T(8,128)(2,1)} %shard_map.105), channel_id=1, source_target_pairs={{0,8},{8,0},{1,9},{9,1},{2,10},{10,2},{3,11},{11,3},{4,12},{12,4},... | collective-permute-start | bytes 7077896 | tf_op jit(solution)/shard_map/ppermute | solution.py:17
  28.1 17.2 %collective-permute-start.10 = (bf16[384,3072]{1,0:T(8,128)(2,1)S(1)}, bf16[384,3072]{1,0:T(8,128)(2,1)}, u32[]{:S(2)}, u32[]{:S(2)}) collective-permute-start(bf16[384,3072]{1,0:T(8,128)(2,1)S(1)} %shard_map.104), channel_id=1, source_target_pairs={{0,8},{8,0},{1,9},{9,1},{2,10},{10,2},{3,11},{11,3},{4,12},{12,4},... | collective-permute-start | bytes 7077896 | tf_op jit(solution)/shard_map/ppermute | solution.py:17
  28.9 7.4 %collective-permute-start.8 = (bf16[192,768]{1,0:T(8,128)(2,1)S(1)}, bf16[192,768]{1,0:T(8,128)(2,1)S(1)}, u32[]{:S(2)}, u32[]{:S(2)}) collective-permute-start(bf16[192,768]{1,0:T(8,128)(2,1)S(1)} %fusion.64), channel_id=1, source_target_pairs={{0,8},{8,0},{1,9},{9,1},{2,10},{10,2},{3,11},{11,3},{4,12},{12,4},... | collective-permute-start | bytes 884744 | tf_op jit(solution)/shard_map/ppermute | solution.py:17
  35.8 38.1 %collective-permute-start.13 = (bf16[384,3072]{1,0:T(8,128)(2,1)}, bf16[384,3072]{1,0:T(8,128)(2,1)}, u32[]{:S(2)}, u32[]{:S(2)}) collective-permute-start(bf16[384,3072]{1,0:T(8,128)(2,1)} %get-tuple-element.35), channel_id=1, source_target_pairs={{0,8},{8,0},{1,9},{9,1},{2,10},{10,2},{3,11},{11,3},{4,12},{12,4},... | collective-permute-start | bytes 7077896 | tf_op jit(solution)/shard_map/ppermute | solution.py:17
  41.4 24.9 %collective-permute-start.15 = (bf16[320,1536]{1,0:T(8,128)(2,1)}, bf16[320,1536]{1,0:T(8,128)(2,1)}, u32[]{:S(2)}, u32[]{:S(2)}) collective-permute-start(bf16[320,1536]{1,0:T(8,128)(2,1)} %fusion.10), channel_id=1, source_target_pairs={{0,1},{1,0},{2,3},{3,2},{4,5},{5,4},{6,7},{7,6},{8,9},{9,8},{10,11... | collective-permute-start | bytes 2949128 | tf_op jit(solution)/shard_map/ppermute | solution.py:151
  41.5 58.0 %collective-permute-start.9 = (bf16[384,3072]{1,0:T(8,128)(2,1)}, bf16[384,3072]{1,0:T(8,128)(2,1)S(1)}, u32[]{:S(2)}, u32[]{:S(2)}) collective-permute-start(bf16[384,3072]{1,0:T(8,128)(2,1)} %get-tuple-element.34), channel_id=1, source_target_pairs={{0,8},{8,0},{1,9},{9,1},{2,10},{10,2},{3,11},{11,3},{4,12},{12,4},... | collective-permute-start | bytes 7077896 | tf_op jit(solution)/shard_map/ppermute | solution.py:17
  47.3 40.0 %collective-permute-start.11 = (bf16[320,1536]{1,0:T(8,128)(2,1)S(1)}, bf16[320,1536]{1,0:T(8,128)(2,1)S(1)}, u32[]{:S(2)}, u32[]{:S(2)}) collective-permute-start(bf16[320,1536]{1,0:T(8,128)(2,1)S(1)} %fusion.8), channel_id=1, source_target_pairs={{0,1},{1,0},{2,3},{3,2},{4,5},{5,4},{6,7},{7,6},{8,9},{9,8},{10,11... | collective-permute-start | bytes 2949128 | tf_op jit(solution)/shard_map/ppermute | solution.py:151
  68.6 21.0 %collective-permute-start.17 = (bf16[320,1536]{1,0:T(8,128)(2,1)S(1)}, bf16[320,1536]{1,0:T(8,128)(2,1)S(1)}, u32[]{:S(2)}, u32[]{:S(2)}) collective-permute-start(bf16[320,1536]{1,0:T(8,128)(2,1)S(1)} %get-tuple-element.54), channel_id=1, source_target_pairs={{0,2},{1,3},{6,4},{7,5},{8,10},{9,11},{14,12},{15,13},{16,18},{17,... | collective-permute-start | bytes 2949128 | tf_op jit(solution)/shard_map/ppermute | solution.py:93
  75.8 32.5 %collective-permute-start.16 = (bf16[320,1536]{1,0:T(8,128)(2,1)S(1)}, bf16[320,1536]{1,0:T(8,128)(2,1)S(1)}, u32[]{:S(2)}, u32[]{:S(2)}) collective-permute-start(bf16[320,1536]{1,0:T(8,128)(2,1)S(1)} %fusion.9), channel_id=1, source_target_pairs={{0,1},{1,0},{2,3},{3,2},{4,5},{5,4},{6,7},{7,6},{8,9},{9,8},{10,11... | collective-permute-start | bytes 2949128 | tf_op jit(solution)/shard_map/ppermute | solution.py:151
  90.2 23.2 %collective-permute-start.18 = (bf16[320,1536]{1,0:T(8,128)(2,1)S(1)}, bf16[320,1536]{1,0:T(8,128)(2,1)S(1)}, u32[]{:S(2)}, u32[]{:S(2)}) collective-permute-start(bf16[320,1536]{1,0:T(8,128)(2,1)S(1)} %select_convert_fusion), channel_id=1, source_target_pairs={{0,2},{1,3},{2,4},{3,5},{8,10},{9,11},{10,12},{11,13},{16,18},{17,... | collective-permute-start | bytes 2949128 | tf_op jit(solution)/shard_map/ppermute | solution.py:93
  94.6 18.7 %collective-permute-start.20 = (bf16[320,1536]{1,0:T(8,128)(2,1)S(1)}, bf16[320,1536]{1,0:T(8,128)(2,1)S(1)}, u32[]{:S(2)}, u32[]{:S(2)}) collective-permute-start(bf16[320,1536]{1,0:T(8,128)(2,1)S(1)} %select_convert_fusion), channel_id=1, source_target_pairs={{6,4},{7,5},{4,2},{5,3},{14,12},{15,13},{12,10},{13,11},{22,20},{2... | collective-permute-start | bytes 2949128 | tf_op jit(solution)/shard_map/ppermute | solution.py:93
  100.8 29.4 %collective-permute-start.12 = (bf16[320,1536]{1,0:T(8,128)(2,1)S(1)}, bf16[320,1536]{1,0:T(8,128)(2,1)}, u32[]{:S(2)}, u32[]{:S(2)}) collective-permute-start(bf16[320,1536]{1,0:T(8,128)(2,1)S(1)} %fusion.7), channel_id=1, source_target_pairs={{0,1},{1,0},{2,3},{3,2},{4,5},{5,4},{6,7},{7,6},{8,9},{9,8},{10,11... | collective-permute-start | bytes 2949128 | tf_op jit(solution)/shard_map/ppermute | solution.py:151
  110.4 13.2 %copy-start = (bf16[192,768]{1,0:T(8,128)(2,1)S(1)}, bf16[192,768]{1,0:T(8,128)(2,1)}, u32[]{:S(2)}) copy-start(bf16[192,768]{1,0:T(8,128)(2,1)} %param.9) | copy-start | bytes 884740
  110.4 17.6 %copy-start.3 = (bf16[1536]{0:T(1024)(128)(2,1)S(1)}, bf16[1536]{0:T(1024)(128)(2,1)}, u32[]{:S(2)}) copy-start(bf16[1536]{0:T(1024)(128)(2,1)} %param.13) | copy-start | bytes 9220
  114.9 24.2 %collective-permute-start.19 = (bf16[320,1536]{1,0:T(8,128)(2,1)}, bf16[320,1536]{1,0:T(8,128)(2,1)}, u32[]{:S(2)}, u32[]{:S(2)}) collective-permute-start(bf16[320,1536]{1,0:T(8,128)(2,1)} %get-tuple-element.36), channel_id=1, source_target_pairs={{0,2},{1,3},{2,4},{3,5},{4,6},{5,7},{8,10},{9,11},{10,12},{11,13},... | collective-permute-start | bytes 2949128 | tf_op jit(solution)/shard_map/ppermute | solution.py:93
  122.2 21.8 %collective-permute-start.21 = (bf16[320,1536]{1,0:T(8,128)(2,1)S(1)}, bf16[320,1536]{1,0:T(8,128)(2,1)}, u32[]{:S(2)}, u32[]{:S(2)}) collective-permute-start(bf16[320,1536]{1,0:T(8,128)(2,1)S(1)} %get-tuple-element.37), channel_id=1, source_target_pairs={{6,4},{7,5},{4,2},{5,3},{2,0},{3,1},{14,12},{15,13},{12,10},{13,11... | collective-permute-start | bytes 2949128 | tf_op jit(solution)/shard_map/ppermute | solution.py:93
  123.5 56.0 %collective-permute-start = (s32[192]{0:T(256)S(1)}, s32[192]{0:T(256)S(1)}, u32[]{:S(2)}, u32[]{:S(2)}) collective-permute-start(s32[192]{0:T(256)S(1)} %copy-done.5), channel_id=1, source_target_pairs={{0,8},{8,0},{1,9},{9,1},{2,10},{10,2},{3,11},{11,3},{4,12},{12,4},... | collective-permute-start | bytes 2312 | tf_op jit(solution)/shard_map/ppermute | solution.py:17
  123.6 56.9 %collective-permute-start.1 = (bf16[32,768]{1,0:T(8,128)(2,1)S(1)}, bf16[32,768]{1,0:T(8,128)(2,1)S(1)}, u32[]{:S(2)}, u32[]{:S(2)}) collective-permute-start(bf16[32,768]{1,0:T(8,128)(2,1)S(1)} %slice.181), channel_id=1, source_target_pairs={{0,8},{8,0},{1,9},{9,1},{2,10},{10,2},{3,11},{11,3},{4,12},{12,4},... | collective-permute-start | bytes 147464 | tf_op jit(solution)/shard_map/ppermute | solution.py:17
  128.1 15.9 %copy-start.2 = (bf16[384,3072]{1,0:T(8,128)(2,1)S(1)}, bf16[384,3072]{1,0:T(8,128)(2,1)}, u32[]{:S(2)}) copy-start(bf16[384,3072]{1,0:T(8,128)(2,1)} %copy-done.1) | copy-start | bytes 7077892
  128.1 22.6 %slice-start.1 = ((s8[18874368]{0:T(1024)(128)(4,1)}), s8[4194304]{0:T(1024)(128)(4,1)S(1)}, s32[]{:S(2)}) async-start(s8[18874368]{0:T(1024)(128)(4,1)} %bitcast.31), calls=%async_computation.1 | async-start | bytes 8388608
  130.2 20.5 %slice-start.2 = ((s8[18874368]{0:T(1024)(128)(4,1)}), s8[4194304]{0:T(1024)(128)(4,1)S(1)}, s32[]{:S(2)}) async-start(s8[18874368]{0:T(1024)(128)(4,1)} %bitcast.31), calls=%async_computation.2 | async-start | bytes 8388608
  130.2 20.5 %slice-start.3 = ((s8[18874368]{0:T(1024)(128)(4,1)}), s8[4194304]{0:T(1024)(128)(4,1)S(1)}, s32[]{:S(2)}) async-start(s8[18874368]{0:T(1024)(128)(4,1)} %bitcast.31), calls=%async_computation.3 | async-start | bytes 8388608
  130.2 20.5 %slice-start.4 = ((s8[18874368]{0:T(1024)(128)(4,1)}), s8[4194304]{0:T(1024)(128)(4,1)S(1)}, s32[]{:S(2)}) async-start(s8[18874368]{0:T(1024)(128)(4,1)} %bitcast.31), calls=%async_computation.4 | async-start | bytes 8388608
  130.2 20.5 %slice-start.5 = ((s8[18874368]{0:T(1024)(128)(4,1)}), s8[2097152]{0:T(1024)(128)(4,1)S(1)}, s32[]{:S(2)}) async-start(s8[18874368]{0:T(1024)(128)(4,1)} %bitcast.31), calls=%async_computation.5 | async-start | bytes 4194304
  151.7 3.8 %collective-permute-start.23 = (f32[160,768]{1,0:T(8,128)S(1)}, f32[160,768]{1,0:T(8,128)S(1)}, u32[]{:S(2)}, u32[]{:S(2)}) collective-permute-start(f32[160,768]{1,0:T(8,128)S(1)} %slice.238), channel_id=1, source_target_pairs={{0,8},{8,0},{1,9},{9,1},{2,10},{10,2},{3,11},{11,3},{4,12},{12,4},... | collective-permute-start | bytes 1474568 | tf_op jit(solution)/shard_map/ppermute | solution.py:17
  152.9 8.4 %collective-permute-start.22 = (f32[160,768]{1,0:T(8,128)S(1)}, f32[160,768]{1,0:T(8,128)S(1)}, u32[]{:S(2)}, u32[]{:S(2)}) collective-permute-start(f32[160,768]{1,0:T(8,128)S(1)} %slice.236), channel_id=1, source_target_pairs={{0,8},{8,0},{1,9},{9,1},{2,10},{10,2},{3,11},{11,3},{4,12},{12,4},... | collective-permute-start | bytes 1474568 | tf_op jit(solution)/shard_map/ppermute | solution.py:17
  154.4 1.9 collective-permute-start.27
  155.5 9.3 %collective-permute-start.26 = (f32[160,768]{1,0:T(8,128)S(1)}, f32[160,768]{1,0:T(8,128)S(1)}, u32[]{:S(2)}, u32[]{:S(2)}) collective-permute-start(f32[160,768]{1,0:T(8,128)S(1)} %slice.240), channel_id=1, source_target_pairs={{0,8},{8,0},{1,9},{9,1},{2,10},{10,2},{3,11},{11,3},{4,12},{12,4},... | collective-permute-start | bytes 1474568 | tf_op jit(solution)/shard_map/ppermute | solution.py:17
  156.3 8.5 %collective-permute-start.24 = (bf16[160,768]{1,0:T(8,128)(2,1)S(1)}, bf16[160,768]{1,0:T(8,128)(2,1)S(1)}, u32[]{:S(2)}, u32[]{:S(2)}) collective-permute-start(bf16[160,768]{1,0:T(8,128)(2,1)S(1)} %fusion.78), channel_id=1, source_target_pairs={{0,1},{1,0},{2,3},{3,2},{4,5},{5,4},{6,7},{7,6},{8,9},{9,8},{10,11... | collective-permute-start | bytes 737288 | tf_op jit(solution)/shard_map/ppermute | solution.py:151
  161.3 8.3 %collective-permute-start.28 = (bf16[160,768]{1,0:T(8,128)(2,1)S(1)}, bf16[160,768]{1,0:T(8,128)(2,1)S(1)}, u32[]{:S(2)}, u32[]{:S(2)}) collective-permute-start(bf16[160,768]{1,0:T(8,128)(2,1)S(1)} %fusion.75), channel_id=1, source_target_pairs={{0,1},{1,0},{2,3},{3,2},{4,5},{5,4},{6,7},{7,6},{8,9},{9,8},{10,11... | collective-permute-start | bytes 737288 | tf_op jit(solution)/shard_map/ppermute | solution.py:151
  164.8 4.9 %collective-permute-start.31 = (f32[160,768]{1,0:T(8,128)S(1)}, f32[160,768]{1,0:T(8,128)S(1)}, u32[]{:S(2)}, u32[]{:S(2)}) collective-permute-start(f32[160,768]{1,0:T(8,128)S(1)} %slice.246), channel_id=1, source_target_pairs={{0,8},{8,0},{1,9},{9,1},{2,10},{10,2},{3,11},{11,3},{4,12},{12,4},... | collective-permute-start | bytes 1474568 | tf_op jit(solution)/shard_map/ppermute | solution.py:17
  164.9 7.5 %collective-permute-start.30 = (f32[160,768]{1,0:T(8,128)S(1)}, f32[160,768]{1,0:T(8,128)S(1)}, u32[]{:S(2)}, u32[]{:S(2)}) collective-permute-start(f32[160,768]{1,0:T(8,128)S(1)} %slice.244), channel_id=1, source_target_pairs={{0,8},{8,0},{1,9},{9,1},{2,10},{10,2},{3,11},{11,3},{4,12},{12,4},... | collective-permute-start | bytes 1474568 | tf_op jit(solution)/shard_map/ppermute | solution.py:17
  169.6 1.9 collective-permute-start.35
  169.7 25.1 %slice-start = ((bf16[192,768]{1,0:T(8,128)(2,1)}), bf16[128,768]{1,0:T(8,128)(2,1)S(1)}, s32[]{:S(2)}) async-start(bf16[192,768]{1,0:T(8,128)(2,1)} %param.9), calls=%async_computation | async-start | bytes 393216 | tf_op jit(solution)/shard_map/slice | solution.py:313
  169.7 11.0 %collective-permute-start.34 = (f32[160,768]{1,0:T(8,128)S(1)}, f32[160,768]{1,0:T(8,128)S(1)}, u32[]{:S(2)}, u32[]{:S(2)}) collective-permute-start(f32[160,768]{1,0:T(8,128)S(1)} %slice.248), channel_id=1, source_target_pairs={{0,8},{8,0},{1,9},{9,1},{2,10},{10,2},{3,11},{11,3},{4,12},{12,4},... | collective-permute-start | bytes 1474568 | tf_op jit(solution)/shard_map/ppermute | solution.py:17
  171.4 8.0 %collective-permute-start.32 = (bf16[160,768]{1,0:T(8,128)(2,1)S(1)}, bf16[160,768]{1,0:T(8,128)(2,1)S(1)}, u32[]{:S(2)}, u32[]{:S(2)}) collective-permute-start(bf16[160,768]{1,0:T(8,128)(2,1)S(1)} %fusion.72), channel_id=1, source_target_pairs={{0,1},{1,0},{2,3},{3,2},{4,5},{5,4},{6,7},{7,6},{8,9},{9,8},{10,11... | collective-permute-start | bytes 737288 | tf_op jit(solution)/shard_map/ppermute | solution.py:151
  172.3 10.5 %collective-permute-start.25 = (bf16[160,768]{1,0:T(8,128)(2,1)S(1)}, bf16[160,768]{1,0:T(8,128)(2,1)S(1)}, u32[]{:S(2)}, u32[]{:S(2)}) collective-permute-start(bf16[160,768]{1,0:T(8,128)(2,1)S(1)} %fusion.80), channel_id=1, source_target_pairs={{0,6},{1,7},{2,4},{3,5},{4,2},{5,3},{6,0},{7,1},{8,14},{9,15},{10,... | collective-permute-start | bytes 737288 | tf_op jit(solution)/shard_map/ppermute | solution.py:93
  179.4 15.4 %collective-permute-start.29 = (bf16[160,768]{1,0:T(8,128)(2,1)S(1)}, bf16[160,768]{1,0:T(8,128)(2,1)S(1)}, u32[]{:S(2)}, u32[]{:S(2)}) collective-permute-start(bf16[160,768]{1,0:T(8,128)(2,1)S(1)} %fusion.77), channel_id=1, source_target_pairs={{0,4},{1,5},{2,6},{3,7},{4,0},{5,1},{6,2},{7,3},{8,12},{9,13},{10,... | collective-permute-start | bytes 737288 | tf_op jit(solution)/shard_map/ppermute | solution.py:93
  179.5 15.3 %collective-permute-start.36 = (bf16[160,768]{1,0:T(8,128)(2,1)S(1)}, bf16[160,768]{1,0:T(8,128)(2,1)S(1)}, u32[]{:S(2)}, u32[]{:S(2)}) collective-permute-start(bf16[160,768]{1,0:T(8,128)(2,1)S(1)} %fusion.65), channel_id=1, source_target_pairs={{0,1},{1,0},{2,3},{3,2},{4,5},{5,4},{6,7},{7,6},{8,9},{9,8},{10,11... | collective-permute-start | bytes 737288 | tf_op jit(solution)/shard_map/ppermute | solution.py:151
  180.5 14.4 %collective-permute-start.33 = (bf16[160,768]{1,0:T(8,128)(2,1)S(1)}, bf16[160,768]{1,0:T(8,128)(2,1)S(1)}, u32[]{:S(2)}, u32[]{:S(2)}) collective-permute-start(bf16[160,768]{1,0:T(8,128)(2,1)S(1)} %fusion.74), channel_id=1, source_target_pairs={{0,2},{1,3},{2,0},{3,1},{4,6},{5,7},{6,4},{7,5},{8,10},{9,11},{10,... | collective-permute-start | bytes 737288 | tf_op jit(solution)/shard_map/ppermute | solution.py:93
  195.2 1.2 collective-permute-start.38
  195.4 1.8 collective-permute-start.37
  (3 other events, 25.5 us)

commit v4 on v3

--- a/solution.py
+++ b/solution.py
@@ -75,7 +75,7 @@
 ACROSS = [(i, i ^ 1) for i in range(8)]
 DIRECT_ORDER = tuple(tuple(z ^ (3 - i) for i in range(4)) for z in range(4))
 ORDER = ((3, 2, 1, 0), (3, 2, 0, 1), (0, 1, 3, 2), (0, 1, 2, 3))
-DEPTH = 2
+DEPTH = 3
 
 
 def along_z(*moves):
@@ -160,6 +160,13 @@
     def step(self):
         step, z, kept = len(self.kept), self.z, self.kept
         sent, own = self.block(step)
+        if step == 0 and not self.direct:
+            cut = sent.shape[0] // 4
+            parts = [own[:cut] + self.across.send(sent[:cut])]
+            parts.append(own[cut:] + self.across.send(sent[cut:]))
+            kept.append(jnp.concatenate(parts, axis=0))
+            self.first = jnp.concatenate([shift(part, ENDS_IN) for part in parts], axis=0)
+            return None
         kept.append(own + self.across.send(sent))
         if self.direct:
             if step < 3:

time: 199 us -> 199 us (level)
  waiting for transfers between devices: 81.1 us -> 90.6 us
  matrix products: 43.9 us -> 37.7 us
  local copies, waits for them, and re-layouts: 12.6 us -> 10.4 us
    ppermute x8 -> x9, waiting for transfers between devices: 31.1 us -> 39.7 us  [shift(): lax.ppermute(array.astype(jnp.bfloat16), 'mp', moves).astype(jnp.float32)]
    dot_general x8, matrix products: 20.5 us -> 14.2 us  [product(): jnp.dot(rows[:, features:], got, preferred_element_type=jnp.float32)]
    dynamic_slice x1, local copies, waits for them, and re-layouts: 6.78 us -> 4.63 us  [lend(): strip = lax.dynamic_slice_in_dim(inner_weight, start, pair, 1)]
    ppermute x8 -> x9, starting transfers between devices: 15.3 us -> 13.5 us  [shift(): lax.ppermute(array.astype(jnp.bfloat16), 'mp', moves).astype(jnp.float32)]
    ppermute x8 -> x9, starting transfers between devices: 7.19 us -> 8.92 us  [send(): self.done.append(lax.ppermute(array, 'mp', ACROSS))]
    ppermute x8 -> x9, waiting for transfers between devices: 48.2 us -> 48.2 us  [send(): self.done.append(lax.ppermute(array, 'mp', ACROSS))]
  transfers between devices with their start and end apart: 39 -> 41, of which waited for: 15 -> 18; matrix products, arithmetic and copies ran while one was open for 30% -> 26% of each run, Pallas kernels for 3% -> 2%
where the time goes in v4:
time: 199 us; the launch traced here: 198 us
  waiting for transfers between devices  90.6 us (46%)
  starting transfers between devices  40.7 us (20%)
  matrix products  37.7 us (19%)
  local copies, waits for them, and re-layouts  10.4 us (5%)
  between operations  7.51 us (4%)
  other arithmetic  7.02 us (4%)
  Pallas kernels  3.69 us (2%)
    ppermute x9, waiting for transfers between devices, send(): self.done.append(lax.ppermute(array, 'mp', ACROSS))  48.2 us
    ppermute x9, waiting for transfers between devices, shift(): lax.ppermute(array.astype(jnp.bfloat16), 'mp', moves).astype(jnp.float32)  39.7 us
    dot_general x8, matrix products, product(): jnp.dot(rows[:, :features], mine, preferred_element_type=jnp.float32)  15.7 us
    dot_general x8, matrix products, product(): jnp.dot(rows[:, features:], got, preferred_element_type=jnp.float32)  14.2 us
    ppermute x9, starting transfers between devices, shift(): lax.ppermute(array.astype(jnp.bfloat16), 'mp', moves).astype(jnp.float32)  13.5 us
    ppermute x9, starting transfers between devices, send(): self.done.append(lax.ppermute(array, 'mp', ACROSS))  8.92 us
    dot_general x8, matrix products, product(): out = jnp.dot(given, weight, preferred_element_type=jnp.float32)  7.67 us
    ppermute x1, starting transfers between devices, eight(): lax.ppermute(other, 'mp', [(4 * e + q, 2 * q + 1 - e) for e in (0, 1) for...  5.77 us
  transfers between devices with their start and end apart: 41, of which 18 were waited for; matrix products, arithmetic and copies ran while one was open for 26% of the time, Pallas kernels for 2%

profile of v4, /device:TPU:0, one launch (start us, length us, event | category | flops | bytes accessed | tf_op | source)
XLA Modules:
  0.0 197.6 jit_solution(3052182793973719365)
XLA Ops:
  1.3 1.0 fusion.88
  3.0 5.8 %collective-permute-start.4 = (bf16[208,384]{1,0:T(8,128)(2,1)S(1)}, bf16[208,384]{1,0:T(8,128)(2,1)S(1)}, u32[]{:S(2)}, u32[]{:S(2)}) collective-permute-start(bf16[208,384]{1,0:T(8,128)(2,1)S(1)} %get-tuple-element.42), channel_id=1, source_target_pairs={{0,1},{1,3},{2,5},{3,7},{4,0},{5,2},{6,4},{7,6},{8,9},{9,11},{10,1... | collective-permute-start | bytes 479240 | tf_op jit(solution)/shard_map/ppermute | solution.py:206
  8.8 1.2 convert_reduce_fusion
  10.0 2.7 %collective-permute-start.2 = (f32[2,192]{1,0:T(2,128)S(1)}, f32[2,192]{1,0:T(2,128)S(1)}, u32[]{:S(2)}, u32[]{:S(2)}) collective-permute-start(f32[2,192]{1,0:T(2,128)S(1)} %pad_maximum_fusion.3), channel_id=1, source_target_pairs={{0,1},{1,0},{2,3},{3,2},{4,5},{5,4},{6,7},{7,6},{8,9},{9,8},{10,11... | collective-permute-start | bytes 4616 | tf_op jit(solution)/shard_map/ppermute | solution.py:210
  16.6 1.3 slice.189
  18.7 1.9 collective-permute-start.6
  20.6 2.4 %collective-permute-start.7 = (f32[2,192]{1,0:T(2,128)S(1)}, f32[2,192]{1,0:T(2,128)S(1)}, u32[]{:S(2)}, u32[]{:S(2)}) collective-permute-start(f32[2,192]{1,0:T(2,128)S(1)} %fusion.132), channel_id=1, source_target_pairs={{0,6},{1,7},{2,4},{3,5},{4,2},{5,3},{6,0},{7,1},{8,14},{9,15},{10,... | collective-permute-start | bytes 4616 | tf_op jit(solution)/shard_map/ppermute | solution.py:214
  23.2 1.8 shard_map.104
  26.3 4.6 %constant_dynamic-slice_fusion.2 = (bf16[384,3072]{1,0:T(8,128)(2,1)S(1)}, bf16[384,3072]{1,0:T(8,128)(2,1)S(1)}) fusion(bf16[384,24576]{1,0:T(8,128)(2,1)} %weight_ref.3, s32[]{:T(128)S(6)} %select_n.163, s32[]{:T(128)S(6)} %select_n.172), kind=kLoop, calls=%fused_computation.184 | loop fusion | bytes 9437192 | tf_op jit(solution)/shard_map/dynamic_slice | solution.py:252
  31.5 1.8 shard_map.105
  34.2 1.9 fusion.42
  36.1 1.9 fusion.54
  38.1 1.9 fusion.39
  40.0 1.9 fusion.48
  42.0 1.9 fusion.7
  44.0 1.0 collective-permute-start.11
  45.0 1.9 fusion.51
  46.9 1.2 collective-permute-start.16
  48.8 1.0 collective-permute-start.14
  49.8 1.9 convolution_add_fusion
  51.7 11.6 %collective-permute-done.11 = bf16[240,1536]{1,0:T(8,128)(2,1)S(1)} collective-permute-done((bf16[240,1536]{1,0:T(8,128)(2,1)S(1)}, bf16[240,1536]{1,0:T(8,128)(2,1)S(1)}, u32[]{:S(2)}, u32[]{:S(2)}) %collective-permute-start.11) | collective-permute-done | bytes 737312 | tf_op jit(solution)/shard_map/ppermute | solution.py:151
  63.6 1.3 collective-permute-start.19
  65.0 3.7 %collective-permute-done.16 = bf16[80,1536]{1,0:T(8,128)(2,1)S(1)} collective-permute-done((bf16[80,1536]{1,0:T(8,128)(2,1)S(1)}, bf16[80,1536]{1,0:T(8,128)(2,1)S(1)}, u32[]{:S(2)}, u32[]{:S(2)}) %collective-permute-start.16) | collective-permute-done | bytes 245792 | tf_op jit(solution)/shard_map/ppermute | solution.py:151
  68.7 1.3 collective-permute-start.18
  71.7 13.0 %collective-permute-done.18 = bf16[80,1536]{1,0:T(8,128)(2,1)S(1)} collective-permute-done((bf16[80,1536]{1,0:T(8,128)(2,1)S(1)}, bf16[80,1536]{1,0:T(8,128)(2,1)S(1)}, u32[]{:S(2)}, u32[]{:S(2)}) %collective-permute-start.18) | collective-permute-done | bytes 245792 | tf_op jit(solution)/shard_map/ppermute | solution.py:93
  84.7 5.0 %collective-permute-done.14 = bf16[320,1536]{1,0:T(8,128)(2,1)S(1)} collective-permute-done((bf16[320,1536]{1,0:T(8,128)(2,1)S(1)}, bf16[320,1536]{1,0:T(8,128)(2,1)S(1)}, u32[]{:S(2)}, u32[]{:S(2)}) %collective-permute-start.14) | collective-permute-done | bytes 983072 | tf_op jit(solution)/shard_map/ppermute | solution.py:151
  90.5 1.4 collective-permute-start.20
  92.8 1.9 fusion.45
  94.7 1.9 fusion.57
  99.0 11.8 %collective-permute-done.17 = bf16[320,1536]{1,0:T(8,128)(2,1)S(1)} collective-permute-done((bf16[320,1536]{1,0:T(8,128)(2,1)S(1)}, bf16[320,1536]{1,0:T(8,128)(2,1)S(1)}, u32[]{:S(2)}, u32[]{:S(2)}) %collective-permute-start.17) | collective-permute-done | bytes 983072 | tf_op jit(solution)/shard_map/ppermute | solution.py:151
  111.6 1.6 add_convert_fusion.1
  113.2 7.2 %collective-permute-start.21 = (bf16[320,1536]{1,0:T(8,128)(2,1)}, bf16[320,1536]{1,0:T(8,128)(2,1)}, u32[]{:S(2)}, u32[]{:S(2)}) collective-permute-start(bf16[320,1536]{1,0:T(8,128)(2,1)} %get-tuple-element.40), channel_id=1, source_target_pairs={{0,2},{1,3},{2,4},{3,5},{4,6},{5,7},{8,10},{9,11},{10,12},{11,13},... | collective-permute-start | bytes 2949128 | tf_op jit(solution)/shard_map/ppermute | solution.py:93
  120.4 1.3 collective-permute-start.23
  126.2 2.1 %fusion.60 = f32[320,1536]{1,0:T(8,128)S(1)} fusion(bf16[384,24576]{1,0:T(8,128)(2,1)} %weight_ref.3, s32[]{:T(128)S(6)} %select_n.162, bf16[320,768]{1,0:T(8,128)(2,1)S(1)} %pad_maximum_fusion), kind=kOutput, calls=%fused_computation.81 | convolution fusion | flops 377487360 | bytes 3391492 | tf_op jit(solution)/shard_map/dot_general | solution.py:264
  128.4 2.7 %collective-permute-done.12 = bf16[320,1536]{1,0:T(8,128)(2,1)} collective-permute-done((bf16[320,1536]{1,0:T(8,128)(2,1)S(1)}, bf16[320,1536]{1,0:T(8,128)(2,1)}, u32[]{:S(2)}, u32[]{:S(2)}) %collective-permute-start.12) | collective-permute-done | bytes 983072 | tf_op jit(solution)/shard_map/ppermute | solution.py:151
  131.1 7.0 %collective-permute-done.21 = bf16[320,1536]{1,0:T(8,128)(2,1)} collective-permute-done((bf16[320,1536]{1,0:T(8,128)(2,1)}, bf16[320,1536]{1,0:T(8,128)(2,1)}, u32[]{:S(2)}, u32[]{:S(2)}) %collective-permute-start.21) | collective-permute-done | bytes 983072 | tf_op jit(solution)/shard_map/ppermute | solution.py:93
  138.1 4.9 %collective-permute-done.23 = bf16[320,1536]{1,0:T(8,128)(2,1)} collective-permute-done((bf16[320,1536]{1,0:T(8,128)(2,1)S(1)}, bf16[320,1536]{1,0:T(8,128)(2,1)}, u32[]{:S(2)}, u32[]{:S(2)}) %collective-permute-start.23) | collective-permute-done | bytes 983072 | tf_op jit(solution)/shard_map/ppermute | solution.py:93
  143.0 6.7 %fusion.28 = bf16[320,1536]{1,0:T(8,128)(2,1)S(1)} fusion(bf16[320,1536]{1,0:T(8,128)(2,1)} %collective-permute-done.23, bf16[320,1536]{1,0:T(8,128)(2,1)} %collective-permute-done.21, bf16[320,1536]{1,0:T(8,128)(2,1)} %collective-permute-done.12, f32[320,1536]{1,0:T(8,128)S(1)} %fusion.60, bf16[384,3072]{1,0:T(8,128)(2,1)S(1)} %copy-done.2, ...), kind=kOutput, calls=%fused_computation.37 | convolution fusion | flops 413368320 | bytes 7331844 | tf_op jit(solution)/shard_map/dot_general | solution.py:266
  150.9 1.0 fusion.24
  157.3 1.0 fusion.16
  159.3 1.0 fusion.12
  160.3 1.2 collective-permute-start.30
  161.5 2.3 %collective-permute-done.26 = bf16[160,768]{1,0:T(8,128)(2,1)S(1)} collective-permute-done((bf16[160,768]{1,0:T(8,128)(2,1)S(1)}, bf16[160,768]{1,0:T(8,128)(2,1)S(1)}, u32[]{:S(2)}, u32[]{:S(2)}) %collective-permute-start.26) | collective-permute-done | bytes 245792 | tf_op jit(solution)/shard_map/ppermute | solution.py:151
  164.5 4.2 %collective-permute-done.30 = bf16[160,768]{1,0:T(8,128)(2,1)S(1)} collective-permute-done((bf16[160,768]{1,0:T(8,128)(2,1)S(1)}, bf16[160,768]{1,0:T(8,128)(2,1)S(1)}, u32[]{:S(2)}, u32[]{:S(2)}) %collective-permute-start.30) | collective-permute-done | bytes 245792 | tf_op jit(solution)/shard_map/ppermute | solution.py:151
  169.4 1.1 collective-permute-done.37
  171.5 7.0 %collective-permute-done.34 = bf16[160,768]{1,0:T(8,128)(2,1)S(1)} collective-permute-done((bf16[160,768]{1,0:T(8,128)(2,1)S(1)}, bf16[160,768]{1,0:T(8,128)(2,1)S(1)}, u32[]{:S(2)}, u32[]{:S(2)}) %collective-permute-start.34) | collective-permute-done | bytes 245792 | tf_op jit(solution)/shard_map/ppermute | solution.py:151
  179.8 1.5 collective-permute-done.27
  181.3 13.2 %collective-permute-done.31 = bf16[160,768]{1,0:T(8,128)(2,1)S(1)} collective-permute-done((bf16[160,768]{1,0:T(8,128)(2,1)S(1)}, bf16[160,768]{1,0:T(8,128)(2,1)S(1)}, u32[]{:S(2)}, u32[]{:S(2)}) %collective-permute-start.31) | collective-permute-done | bytes 245792 | tf_op jit(solution)/shard_map/ppermute | solution.py:93
  (143 shorter events, 29.0 us)
Async XLA Ops:
  2.4 16.2 %collective-permute-start.3 = (bf16[208,384]{1,0:T(8,128)(2,1)S(1)}, bf16[208,384]{1,0:T(8,128)(2,1)S(1)}, u32[]{:S(2)}, u32[]{:S(2)}) collective-permute-start(bf16[208,384]{1,0:T(8,128)(2,1)S(1)} %get-tuple-element.43), channel_id=1, source_target_pairs={{0,0},{1,2},{2,4},{3,6},{4,1},{5,3},{6,5},{7,7},{8,8},{9,10},{10,1... | collective-permute-start | bytes 479240 | tf_op jit(solution)/shard_map/ppermute | solution.py:205
  3.0 15.6 %collective-permute-start.4 = (bf16[208,384]{1,0:T(8,128)(2,1)S(1)}, bf16[208,384]{1,0:T(8,128)(2,1)S(1)}, u32[]{:S(2)}, u32[]{:S(2)}) collective-permute-start(bf16[208,384]{1,0:T(8,128)(2,1)S(1)} %get-tuple-element.42), channel_id=1, source_target_pairs={{0,1},{1,3},{2,5},{3,7},{4,0},{5,2},{6,4},{7,6},{8,9},{9,11},{10,1... | collective-permute-start | bytes 479240 | tf_op jit(solution)/shard_map/ppermute | solution.py:206
  10.0 8.6 %collective-permute-start.2 = (f32[2,192]{1,0:T(2,128)S(1)}, f32[2,192]{1,0:T(2,128)S(1)}, u32[]{:S(2)}, u32[]{:S(2)}) collective-permute-start(f32[2,192]{1,0:T(2,128)S(1)} %pad_maximum_fusion.3), channel_id=1, source_target_pairs={{0,1},{1,0},{2,3},{3,2},{4,5},{5,4},{6,7},{7,6},{8,9},{9,8},{10,11... | collective-permute-start | bytes 4616 | tf_op jit(solution)/shard_map/ppermute | solution.py:210
  18.6 6.5 %collective-permute-start.5 = (f32[2,192]{1,0:T(2,128)S(1)}, f32[2,192]{1,0:T(2,128)S(1)}, u32[]{:S(2)}, u32[]{:S(2)}) collective-permute-start(f32[2,192]{1,0:T(2,128)S(1)} %fusion.132), channel_id=1, source_target_pairs={{0,2},{1,3},{2,0},{3,1},{4,6},{5,7},{6,4},{7,5},{8,10},{9,11},{10,... | collective-permute-start | bytes 4616 | tf_op jit(solution)/shard_map/ppermute | solution.py:214
  18.7 6.5 %collective-permute-start.6 = (f32[2,192]{1,0:T(2,128)S(1)}, f32[2,192]{1,0:T(2,128)S(1)}, u32[]{:S(2)}, u32[]{:S(2)}) collective-permute-start(f32[2,192]{1,0:T(2,128)S(1)} %fusion.132), channel_id=1, source_target_pairs={{0,4},{1,5},{2,6},{3,7},{4,0},{5,1},{6,2},{7,3},{8,12},{9,13},{10,... | collective-permute-start | bytes 4616 | tf_op jit(solution)/shard_map/ppermute | solution.py:214
  20.6 5.4 %collective-permute-start.7 = (f32[2,192]{1,0:T(2,128)S(1)}, f32[2,192]{1,0:T(2,128)S(1)}, u32[]{:S(2)}, u32[]{:S(2)}) collective-permute-start(f32[2,192]{1,0:T(2,128)S(1)} %fusion.132), channel_id=1, source_target_pairs={{0,6},{1,7},{2,4},{3,5},{4,2},{5,3},{6,0},{7,1},{8,14},{9,15},{10,... | collective-permute-start | bytes 4616 | tf_op jit(solution)/shard_map/ppermute | solution.py:214
  25.1 16.9 %collective-permute-start.10 = (bf16[384,3072]{1,0:T(8,128)(2,1)S(1)}, bf16[384,3072]{1,0:T(8,128)(2,1)}, u32[]{:S(2)}, u32[]{:S(2)}) collective-permute-start(bf16[384,3072]{1,0:T(8,128)(2,1)S(1)} %shard_map.104), channel_id=1, source_target_pairs={{0,8},{8,0},{1,9},{9,1},{2,10},{10,2},{3,11},{11,3},{4,12},{12,4},... | collective-permute-start | bytes 7077896 | tf_op jit(solution)/shard_map/ppermute | solution.py:17
  26.2 7.7 %collective-permute-start.8 = (bf16[192,768]{1,0:T(8,128)(2,1)S(1)}, bf16[192,768]{1,0:T(8,128)(2,1)S(1)}, u32[]{:S(2)}, u32[]{:S(2)}) collective-permute-start(bf16[192,768]{1,0:T(8,128)(2,1)S(1)} %fusion.65), channel_id=1, source_target_pairs={{0,8},{8,0},{1,9},{9,1},{2,10},{10,2},{3,11},{11,3},{4,12},{12,4},... | collective-permute-start | bytes 884744 | tf_op jit(solution)/shard_map/ppermute | solution.py:17
  30.9 39.1 %collective-permute-start.15 = (bf16[384,3072]{1,0:T(8,128)(2,1)S(1)}, bf16[384,3072]{1,0:T(8,128)(2,1)S(1)}, u32[]{:S(2)}, u32[]{:S(2)}) collective-permute-start(bf16[384,3072]{1,0:T(8,128)(2,1)S(1)} %get-tuple-element.39), channel_id=1, source_target_pairs={{0,8},{8,0},{1,9},{9,1},{2,10},{10,2},{3,11},{11,3},{4,12},{12,4},... | collective-permute-start | bytes 7077896 | tf_op jit(solution)/shard_map/ppermute | solution.py:17
  33.3 14.8 %collective-permute-start.13 = (bf16[384,3072]{1,0:T(8,128)(2,1)S(1)}, bf16[384,3072]{1,0:T(8,128)(2,1)S(1)}, u32[]{:S(2)}, u32[]{:S(2)}) collective-permute-start(bf16[384,3072]{1,0:T(8,128)(2,1)S(1)} %shard_map.105), channel_id=1, source_target_pairs={{0,8},{8,0},{1,9},{9,1},{2,10},{10,2},{3,11},{11,3},{4,12},{12,4},... | collective-permute-start | bytes 7077896 | tf_op jit(solution)/shard_map/ppermute | solution.py:17
  33.4 63.3 %collective-permute-start.9 = (bf16[384,3072]{1,0:T(8,128)(2,1)S(1)}, bf16[384,3072]{1,0:T(8,128)(2,1)S(1)}, u32[]{:S(2)}, u32[]{:S(2)}) collective-permute-start(bf16[384,3072]{1,0:T(8,128)(2,1)S(1)} %get-tuple-element.38), channel_id=1, source_target_pairs={{0,8},{8,0},{1,9},{9,1},{2,10},{10,2},{3,11},{11,3},{4,12},{12,4},... | collective-permute-start | bytes 7077896 | tf_op jit(solution)/shard_map/ppermute | solution.py:17
  44.0 19.4 %collective-permute-start.11 = (bf16[240,1536]{1,0:T(8,128)(2,1)S(1)}, bf16[240,1536]{1,0:T(8,128)(2,1)S(1)}, u32[]{:S(2)}, u32[]{:S(2)}) collective-permute-start(bf16[240,1536]{1,0:T(8,128)(2,1)S(1)} %slice.253), channel_id=1, source_target_pairs={{0,1},{1,0},{2,3},{3,2},{4,5},{5,4},{6,7},{7,6},{8,9},{9,8},{10,11... | collective-permute-start | bytes 2211848 | tf_op jit(solution)/shard_map/ppermute | solution.py:151
  46.9 21.7 %collective-permute-start.16 = (bf16[80,1536]{1,0:T(8,128)(2,1)S(1)}, bf16[80,1536]{1,0:T(8,128)(2,1)S(1)}, u32[]{:S(2)}, u32[]{:S(2)}) collective-permute-start(bf16[80,1536]{1,0:T(8,128)(2,1)S(1)} %slice.254), channel_id=1, source_target_pairs={{0,1},{1,0},{2,3},{3,2},{4,5},{5,4},{6,7},{7,6},{8,9},{9,8},{10,11... | collective-permute-start | bytes 737288 | tf_op jit(solution)/shard_map/ppermute | solution.py:151
  48.8 40.9 %collective-permute-start.14 = (bf16[320,1536]{1,0:T(8,128)(2,1)S(1)}, bf16[320,1536]{1,0:T(8,128)(2,1)S(1)}, u32[]{:S(2)}, u32[]{:S(2)}) collective-permute-start(bf16[320,1536]{1,0:T(8,128)(2,1)S(1)} %fusion.8), channel_id=1, source_target_pairs={{0,1},{1,0},{2,3},{3,2},{4,5},{5,4},{6,7},{7,6},{8,9},{9,8},{10,11... | collective-permute-start | bytes 2949128 | tf_op jit(solution)/shard_map/ppermute | solution.py:151
  63.6 26.1 %collective-permute-start.19 = (bf16[240,1536]{1,0:T(8,128)(2,1)S(1)}, bf16[240,1536]{1,0:T(8,128)(2,1)S(1)}, u32[]{:S(2)}, u32[]{:S(2)}) collective-permute-start(bf16[240,1536]{1,0:T(8,128)(2,1)S(1)} %get-tuple-element.36), channel_id=1, source_target_pairs={{0,2},{1,3},{6,4},{7,5},{8,10},{9,11},{14,12},{15,13},{16,18},{17,... | collective-permute-start | bytes 2211848 | tf_op jit(solution)/shard_map/ppermute | solution.py:93
  68.7 16.0 %collective-permute-start.18 = (bf16[80,1536]{1,0:T(8,128)(2,1)S(1)}, bf16[80,1536]{1,0:T(8,128)(2,1)S(1)}, u32[]{:S(2)}, u32[]{:S(2)}) collective-permute-start(bf16[80,1536]{1,0:T(8,128)(2,1)S(1)} %get-tuple-element.34), channel_id=1, source_target_pairs={{0,2},{1,3},{6,4},{7,5},{8,10},{9,11},{14,12},{15,13},{16,18},{17,... | collective-permute-start | bytes 737288 | tf_op jit(solution)/shard_map/ppermute | solution.py:93
  70.7 40.0 %collective-permute-start.17 = (bf16[320,1536]{1,0:T(8,128)(2,1)S(1)}, bf16[320,1536]{1,0:T(8,128)(2,1)S(1)}, u32[]{:S(2)}, u32[]{:S(2)}) collective-permute-start(bf16[320,1536]{1,0:T(8,128)(2,1)S(1)} %fusion.9), channel_id=1, source_target_pairs={{0,1},{1,0},{2,3},{3,2},{4,5},{5,4},{6,7},{7,6},{8,9},{9,8},{10,11... | collective-permute-start | bytes 2949128 | tf_op jit(solution)/shard_map/ppermute | solution.py:151
  90.5 21.1 %collective-permute-start.20 = (bf16[320,1536]{1,0:T(8,128)(2,1)S(1)}, bf16[320,1536]{1,0:T(8,128)(2,1)S(1)}, u32[]{:S(2)}, u32[]{:S(2)}) collective-permute-start(bf16[320,1536]{1,0:T(8,128)(2,1)S(1)} %get-tuple-element.58), channel_id=1, source_target_pairs={{0,2},{1,3},{2,4},{3,5},{8,10},{9,11},{10,12},{11,13},{16,18},{17,... | collective-permute-start | bytes 2949128 | tf_op jit(solution)/shard_map/ppermute | solution.py:93
  91.9 19.7 %collective-permute-start.22 = (bf16[320,1536]{1,0:T(8,128)(2,1)S(1)}, bf16[320,1536]{1,0:T(8,128)(2,1)S(1)}, u32[]{:S(2)}, u32[]{:S(2)}) collective-permute-start(bf16[320,1536]{1,0:T(8,128)(2,1)S(1)} %get-tuple-element.58), channel_id=1, source_target_pairs={{6,4},{7,5},{4,2},{5,3},{14,12},{15,13},{12,10},{13,11},{22,20},{2... | collective-permute-start | bytes 2949128 | tf_op jit(solution)/shard_map/ppermute | solution.py:93
  98.1 33.0 %collective-permute-start.12 = (bf16[320,1536]{1,0:T(8,128)(2,1)S(1)}, bf16[320,1536]{1,0:T(8,128)(2,1)}, u32[]{:S(2)}, u32[]{:S(2)}) collective-permute-start(bf16[320,1536]{1,0:T(8,128)(2,1)S(1)} %fusion.6), channel_id=1, source_target_pairs={{0,1},{1,0},{2,3},{3,2},{4,5},{5,4},{6,7},{7,6},{8,9},{9,8},{10,11... | collective-permute-start | bytes 2949128 | tf_op jit(solution)/shard_map/ppermute | solution.py:151
  113.2 24.9 %collective-permute-start.21 = (bf16[320,1536]{1,0:T(8,128)(2,1)}, bf16[320,1536]{1,0:T(8,128)(2,1)}, u32[]{:S(2)}, u32[]{:S(2)}) collective-permute-start(bf16[320,1536]{1,0:T(8,128)(2,1)} %get-tuple-element.40), channel_id=1, source_target_pairs={{0,2},{1,3},{2,4},{3,5},{4,6},{5,7},{8,10},{9,11},{10,12},{11,13},... | collective-permute-start | bytes 2949128 | tf_op jit(solution)/shard_map/ppermute | solution.py:93
  120.4 22.6 %collective-permute-start.23 = (bf16[320,1536]{1,0:T(8,128)(2,1)S(1)}, bf16[320,1536]{1,0:T(8,128)(2,1)}, u32[]{:S(2)}, u32[]{:S(2)}) collective-permute-start(bf16[320,1536]{1,0:T(8,128)(2,1)S(1)} %get-tuple-element.41), channel_id=1, source_target_pairs={{6,4},{7,5},{4,2},{5,3},{2,0},{3,1},{14,12},{15,13},{12,10},{13,11... | collective-permute-start | bytes 2949128 | tf_op jit(solution)/shard_map/ppermute | solution.py:93
  121.7 56.9 %collective-permute-start = (s32[192]{0:T(256)S(1)}, s32[192]{0:T(256)S(1)}, u32[]{:S(2)}, u32[]{:S(2)}) collective-permute-start(s32[192]{0:T(256)S(1)} %copy-done.5), channel_id=1, source_target_pairs={{0,8},{8,0},{1,9},{9,1},{2,10},{10,2},{3,11},{11,3},{4,12},{12,4},... | collective-permute-start | bytes 2312 | tf_op jit(solution)/shard_map/ppermute | solution.py:17
  121.8 57.7 %collective-permute-start.1 = (bf16[32,768]{1,0:T(8,128)(2,1)S(1)}, bf16[32,768]{1,0:T(8,128)(2,1)S(1)}, u32[]{:S(2)}, u32[]{:S(2)}) collective-permute-start(bf16[32,768]{1,0:T(8,128)(2,1)S(1)} %slice.195), channel_id=1, source_target_pairs={{0,8},{8,0},{1,9},{9,1},{2,10},{10,2},{3,11},{11,3},{4,12},{12,4},... | collective-permute-start | bytes 147464 | tf_op jit(solution)/shard_map/ppermute | solution.py:17
  126.2 16.8 %copy-start.2 = (bf16[384,3072]{1,0:T(8,128)(2,1)S(1)}, bf16[384,3072]{1,0:T(8,128)(2,1)}, u32[]{:S(2)}) copy-start(bf16[384,3072]{1,0:T(8,128)(2,1)} %copy-done.1) | copy-start | bytes 7077892
  126.2 23.5 %slice-start.1 = ((s8[18874368]{0:T(1024)(128)(4,1)}), s8[4194304]{0:T(1024)(128)(4,1)S(1)}, s32[]{:S(2)}) async-start(s8[18874368]{0:T(1024)(128)(4,1)} %bitcast.31), calls=%async_computation.1 | async-start | bytes 8388608
  128.3 21.4 %slice-start.2 = ((s8[18874368]{0:T(1024)(128)(4,1)}), s8[4194304]{0:T(1024)(128)(4,1)S(1)}, s32[]{:S(2)}) async-start(s8[18874368]{0:T(1024)(128)(4,1)} %bitcast.31), calls=%async_computation.2 | async-start | bytes 8388608
  128.3 21.4 %slice-start.3 = ((s8[18874368]{0:T(1024)(128)(4,1)}), s8[4194304]{0:T(1024)(128)(4,1)S(1)}, s32[]{:S(2)}) async-start(s8[18874368]{0:T(1024)(128)(4,1)} %bitcast.31), calls=%async_computation.3 | async-start | bytes 8388608
  128.3 21.4 %slice-start.4 = ((s8[18874368]{0:T(1024)(128)(4,1)}), s8[4194304]{0:T(1024)(128)(4,1)S(1)}, s32[]{:S(2)}) async-start(s8[18874368]{0:T(1024)(128)(4,1)} %bitcast.31), calls=%async_computation.4 | async-start | bytes 8388608
  128.3 21.4 %slice-start.5 = ((s8[18874368]{0:T(1024)(128)(4,1)}), s8[2097152]{0:T(1024)(128)(4,1)S(1)}, s32[]{:S(2)}) async-start(s8[18874368]{0:T(1024)(128)(4,1)} %bitcast.31), calls=%async_computation.5 | async-start | bytes 4194304
  150.8 3.8 %collective-permute-start.25 = (f32[160,768]{1,0:T(8,128)S(1)}, f32[160,768]{1,0:T(8,128)S(1)}, u32[]{:S(2)}, u32[]{:S(2)}) collective-permute-start(f32[160,768]{1,0:T(8,128)S(1)} %slice.260), channel_id=1, source_target_pairs={{0,8},{8,0},{1,9},{9,1},{2,10},{10,2},{3,11},{11,3},{4,12},{12,4},... | collective-permute-start | bytes 1474568 | tf_op jit(solution)/shard_map/ppermute | solution.py:17
  151.9 8.4 %collective-permute-start.24 = (f32[160,768]{1,0:T(8,128)S(1)}, f32[160,768]{1,0:T(8,128)S(1)}, u32[]{:S(2)}, u32[]{:S(2)}) collective-permute-start(f32[160,768]{1,0:T(8,128)S(1)} %slice.258), channel_id=1, source_target_pairs={{0,8},{8,0},{1,9},{9,1},{2,10},{10,2},{3,11},{11,3},{4,12},{12,4},... | collective-permute-start | bytes 1474568 | tf_op jit(solution)/shard_map/ppermute | solution.py:17
  153.4 1.9 collective-permute-start.29
  154.6 9.3 %collective-permute-start.28 = (f32[160,768]{1,0:T(8,128)S(1)}, f32[160,768]{1,0:T(8,128)S(1)}, u32[]{:S(2)}, u32[]{:S(2)}) collective-permute-start(f32[160,768]{1,0:T(8,128)S(1)} %slice.262), channel_id=1, source_target_pairs={{0,8},{8,0},{1,9},{9,1},{2,10},{10,2},{3,11},{11,3},{4,12},{12,4},... | collective-permute-start | bytes 1474568 | tf_op jit(solution)/shard_map/ppermute | solution.py:17
  155.4 8.4 %collective-permute-start.26 = (bf16[160,768]{1,0:T(8,128)(2,1)S(1)}, bf16[160,768]{1,0:T(8,128)(2,1)S(1)}, u32[]{:S(2)}, u32[]{:S(2)}) collective-permute-start(bf16[160,768]{1,0:T(8,128)(2,1)S(1)} %fusion.79), channel_id=1, source_target_pairs={{0,1},{1,0},{2,3},{3,2},{4,5},{5,4},{6,7},{7,6},{8,9},{9,8},{10,11... | collective-permute-start | bytes 737288 | tf_op jit(solution)/shard_map/ppermute | solution.py:151
  160.3 8.3 %collective-permute-start.30 = (bf16[160,768]{1,0:T(8,128)(2,1)S(1)}, bf16[160,768]{1,0:T(8,128)(2,1)S(1)}, u32[]{:S(2)}, u32[]{:S(2)}) collective-permute-start(bf16[160,768]{1,0:T(8,128)(2,1)S(1)} %fusion.76), channel_id=1, source_target_pairs={{0,1},{1,0},{2,3},{3,2},{4,5},{5,4},{6,7},{7,6},{8,9},{9,8},{10,11... | collective-permute-start | bytes 737288 | tf_op jit(solution)/shard_map/ppermute | solution.py:151
  163.8 4.9 %collective-permute-start.33 = (f32[160,768]{1,0:T(8,128)S(1)}, f32[160,768]{1,0:T(8,128)S(1)}, u32[]{:S(2)}, u32[]{:S(2)}) collective-permute-start(f32[160,768]{1,0:T(8,128)S(1)} %slice.268), channel_id=1, source_target_pairs={{0,8},{8,0},{1,9},{9,1},{2,10},{10,2},{3,11},{11,3},{4,12},{12,4},... | collective-permute-start | bytes 1474568 | tf_op jit(solution)/shard_map/ppermute | solution.py:17
  163.9 7.5 %collective-permute-start.32 = (f32[160,768]{1,0:T(8,128)S(1)}, f32[160,768]{1,0:T(8,128)S(1)}, u32[]{:S(2)}, u32[]{:S(2)}) collective-permute-start(f32[160,768]{1,0:T(8,128)S(1)} %slice.266), channel_id=1, source_target_pairs={{0,8},{8,0},{1,9},{9,1},{2,10},{10,2},{3,11},{11,3},{4,12},{12,4},... | collective-permute-start | bytes 1474568 | tf_op jit(solution)/shard_map/ppermute | solution.py:17
  168.6 1.9 collective-permute-start.37
  168.7 25.8 %slice-start = ((bf16[192,768]{1,0:T(8,128)(2,1)}), bf16[128,768]{1,0:T(8,128)(2,1)S(1)}, s32[]{:S(2)}) async-start(bf16[192,768]{1,0:T(8,128)(2,1)} %param.9), calls=%async_computation | async-start | bytes 393216 | tf_op jit(solution)/shard_map/slice | solution.py:320
  168.7 11.1 %collective-permute-start.36 = (f32[160,768]{1,0:T(8,128)S(1)}, f32[160,768]{1,0:T(8,128)S(1)}, u32[]{:S(2)}, u32[]{:S(2)}) collective-permute-start(f32[160,768]{1,0:T(8,128)S(1)} %slice.270), channel_id=1, source_target_pairs={{0,8},{8,0},{1,9},{9,1},{2,10},{10,2},{3,11},{11,3},{4,12},{12,4},... | collective-permute-start | bytes 1474568 | tf_op jit(solution)/shard_map/ppermute | solution.py:17
  170.5 8.0 %collective-permute-start.34 = (bf16[160,768]{1,0:T(8,128)(2,1)S(1)}, bf16[160,768]{1,0:T(8,128)(2,1)S(1)}, u32[]{:S(2)}, u32[]{:S(2)}) collective-permute-start(bf16[160,768]{1,0:T(8,128)(2,1)S(1)} %fusion.73), channel_id=1, source_target_pairs={{0,1},{1,0},{2,3},{3,2},{4,5},{5,4},{6,7},{7,6},{8,9},{9,8},{10,11... | collective-permute-start | bytes 737288 | tf_op jit(solution)/shard_map/ppermute | solution.py:151
  171.4 9.9 %collective-permute-start.27 = (bf16[160,768]{1,0:T(8,128)(2,1)S(1)}, bf16[160,768]{1,0:T(8,128)(2,1)S(1)}, u32[]{:S(2)}, u32[]{:S(2)}) collective-permute-start(bf16[160,768]{1,0:T(8,128)(2,1)S(1)} %fusion.81), channel_id=1, source_target_pairs={{0,6},{1,7},{2,4},{3,5},{4,2},{5,3},{6,0},{7,1},{8,14},{9,15},{10,... | collective-permute-start | bytes 737288 | tf_op jit(solution)/shard_map/ppermute | solution.py:93
  178.5 16.0 %collective-permute-start.31 = (bf16[160,768]{1,0:T(8,128)(2,1)S(1)}, bf16[160,768]{1,0:T(8,128)(2,1)S(1)}, u32[]{:S(2)}, u32[]{:S(2)}) collective-permute-start(bf16[160,768]{1,0:T(8,128)(2,1)S(1)} %fusion.78), channel_id=1, source_target_pairs={{0,4},{1,5},{2,6},{3,7},{4,0},{5,1},{6,2},{7,3},{8,12},{9,13},{10,... | collective-permute-start | bytes 737288 | tf_op jit(solution)/shard_map/ppermute | solution.py:93
  178.6 15.9 %collective-permute-start.38 = (bf16[160,768]{1,0:T(8,128)(2,1)S(1)}, bf16[160,768]{1,0:T(8,128)(2,1)S(1)}, u32[]{:S(2)}, u32[]{:S(2)}) collective-permute-start(bf16[160,768]{1,0:T(8,128)(2,1)S(1)} %fusion.66), channel_id=1, source_target_pairs={{0,1},{1,0},{2,3},{3,2},{4,5},{5,4},{6,7},{7,6},{8,9},{9,8},{10,11... | collective-permute-start | bytes 737288 | tf_op jit(solution)/shard_map/ppermute | solution.py:151
  179.5 15.0 %collective-permute-start.35 = (bf16[160,768]{1,0:T(8,128)(2,1)S(1)}, bf16[160,768]{1,0:T(8,128)(2,1)S(1)}, u32[]{:S(2)}, u32[]{:S(2)}) collective-permute-start(bf16[160,768]{1,0:T(8,128)(2,1)S(1)} %fusion.75), channel_id=1, source_target_pairs={{0,2},{1,3},{2,0},{3,1},{4,6},{5,7},{6,4},{7,5},{8,10},{9,11},{10,... | collective-permute-start | bytes 737288 | tf_op jit(solution)/shard_map/ppermute | solution.py:93
  194.9 1.2 collective-permute-start.40
  195.1 1.8 collective-permute-start.39
  (5 other events, 47.1 us)
